TPU v7x, 128 devices: a whole 4x4x4 slice. The times are simulated.
128 devices in a mesh: lat: 16 (over y, x_hi, core), lon: 8 (over z, x_lo).
Axes of the slice: x: 4 (x_hi: 2, x_lo: 2; x = x_hi * 2 + x_lo), y: 4, z: 4, core: 2. Of those that a mesh axis runs over, the one named last changes fastest.
Arguments:
- state: float32 [3, 1440, 256, 128], P(None, 'lon', 'lat'), may hold values from -6 to 6
- cutoffs: int32 [256], P('lat'), may hold values from 32 to 180, as said below
Outputs:
- updated: float32 [3, 1440, 256, 128], P(None, 'lon', 'lat')
Inputs may be any that keep to these rules, and one draw needn't show every extreme that they name: `cutoffs`: only rows poleward of 45 degrees read their cutoff.
All inputs are finite; a program needn't handle non-finite values.
Results may differ from a plain program's by a relative error of at most 0.00011.
Values sent between devices are 32-bit elements; how exact they have to be, the bound alone decides.
No kernel may reach another device: no remote copies, remote signals or barrier semaphores. Data moves between devices by JAX's collectives and lax.ppermute only.
A program may use at most 128 MiB of HBM per device.

v0:
```python
import functools

import jax
import jax.numpy as jnp
import numpy as np
from jax import lax
from jax.experimental import pallas as pl
from jax.experimental.pallas import tpu as pltpu
from jax.sharding import PartitionSpec as P

SUBSTEPS = 2
HALO = 1 + 2 * SUBSTEPS
ADV = 0.5
SOUND = 0.8
CAP = 2.0
LEAD = 16
GROUP = 8
MIB = 1024 * 1024

f32 = jnp.float32
bf16 = jnp.bfloat16


def params(mib):
    return pltpu.CompilerParams(vmem_limit_bytes=mib * MIB)


def vmem():
    return pl.BlockSpec(memory_space=pltpu.VMEM)


def smem():
    return pl.BlockSpec(memory_space=pltpu.SMEM)


def edge_row(d):
    return jnp.where(d < 4, d, d + 8)


def inner_row(d):
    return d + 4


EDGE = [d if d < 4 else d + 8 for d in range(GROUP)]
INNER = [d + 4 for d in range(GROUP)]


def padded(cols):
    return -(-cols // 8) * 8


def window(cols):
    return -(-(8 + cols + HALO) // 8) * 8


def cost(micros):
    return pl.CostEstimate(flops=0, bytes_accessed=int(micros * 3.69e6), transcendentals=0)


def any_space():
    return pl.BlockSpec(memory_space=pltpu.MemorySpace.HBM)


def send_kernel(cols, rows, x_ref, west_ref, east_ref, _, north_ref, south_ref, hold, sem):
    loads = [pltpu.make_async_copy(x_ref.at[c], hold.at[c], sem.at[c]) for c in range(3)]
    for copy in loads:
        copy.start()

    def put(ref, at, c, r):
        ref[at, pl.ds(8, cols)] = hold[c, pl.ds(r, cols, stride=rows), :]
        ref[at, pl.ds(8 - HALO, HALO)] = west_ref[c, pl.ds(r, HALO, stride=rows), :]
        ref[at, pl.ds(8 + cols, HALO)] = east_ref[c, pl.ds(r, HALO, stride=rows), :]

    top = rows - HALO + 1
    for c in range(3):
        loads[c].wait()
        for k in range(HALO - 1):
            put(north_ref, (HALO - 1) * c + k, c, k)
            put(south_ref, (HALO - 1) * c + k, c, top + k)
    put(north_ref, 3 * (HALO - 1), 2, HALO - 1)
    put(south_ref, 3 * (HALO - 1), 2, rows - HALO)


def row_sends(flat, west, east_, after, cols, rows):
    lev = flat.shape[-1]
    edge = jax.ShapeDtypeStruct((3 * (HALO - 1) + 1, window(cols), lev), f32)
    return pl.pallas_call(
        functools.partial(send_kernel, cols, rows),
        in_specs=[any_space(), vmem(), vmem(), any_space()],
        out_specs=[vmem()] * 2,
        out_shape=[edge, edge],
        scratch_shapes=[pltpu.VMEM(flat.shape, f32), pltpu.SemaphoreType.DMA((3,))],
        compiler_params=params(60),
        cost_estimate=cost(4),
    )(flat, west, east_, after)


def east(W, r):
    cols = W.shape[1] - 16
    return W[r, pl.ds(9, cols)] - W[r, pl.ds(7, cols)]


def stage_steps(metric_ref, base, U, V, T, A, B, C, keep):
    mid = pl.ds(8, U.shape[1] - 16)

    def metric(i):
        return metric_ref[i + (HALO - base)]

    def advect(i, fields=None):
        mu = metric(i) * (0.5 * ADV) * U[i, mid]
        nv = (0.5 * ADV) * V[i, mid]
        for W, out in fields or ((U, A), (V, B), (T, C)):
            out[i, mid] = W[i, mid] - (mu * east(W, i) + nv * (W[i + 1, mid] - W[i - 1, mid]))

    def advect_theta(i):
        advect(i, ((T, C),))

    def wind_u(i):
        A[i, mid] = A[i, mid] - (metric(i) * (0.5 * SOUND)) * east(C, i)

    def wind_v(i):
        B[i, mid] = keep(i, B[i, mid] - (0.5 * SOUND) * (C[i + 1, mid] - C[i - 1, mid]))

    def theta(i):
        m = metric(i) * (0.5 * SOUND)
        C[i, mid] = keep(i, C[i, mid] - (m * east(A, i) + (0.5 * SOUND) * (B[i + 1, mid] - B[i - 1, mid])))

    return advect, advect_theta, wind_u, wind_v, theta


def sweep(fn, *spans):
    for lo, hi in spans:

        def step(i, carry):
            fn(i)
            return carry

        lax.fori_loop(lo, hi, step, 0)


def inner_kernel(
    cols, rows, metric_ref, x_ref, west_ref, east_ref, _, u_ref, v_ref, theta_ref, rim_ref, raw_ref, *scratch
):
    U, V, T, A, B, C, hold, sem, out_sem = scratch
    own = slice(LEAD, LEAD + cols)
    wide = pl.ds(LEAD - 8, window(cols))
    loads = [pltpu.make_async_copy(x_ref.at[c], hold.at[c], sem.at[c]) for c in range(3)]
    for copy in loads:
        copy.start()
    outs = []
    for c, W in enumerate((U, V, T)):
        loads[c].wait()

        def fill(r, carry, c=c, W=W):
            W[r, own] = hold[c, pl.ds(r, cols, stride=rows), :]
            W[r, pl.ds(LEAD - HALO, HALO)] = west_ref[c, pl.ds(r, HALO, stride=rows), :]
            W[r, pl.ds(LEAD + cols, HALO)] = east_ref[c, pl.ds(r, HALO, stride=rows), :]
            return carry

        lax.fori_loop(0, rows, fill, 0)
        for k, at in ((0, 0), (1, rows - 2)):
            outs.append((W.at[pl.ds(at, 2), wide], raw_ref.at[c, pl.ds(2 * k, 2)]))
    advect, _, wind_u, wind_v, theta = stage_steps(metric_ref, 0, U, V, T, A, B, C, lambda r, x: x)
    sweep(advect, (1, rows - 1))
    sweep(wind_u, (1, rows - 1))
    sweep(wind_v, (2, rows - 2))
    sweep(theta, (3, rows - 3))
    sweep(wind_u, (3, rows - 3))
    sweep(wind_v, (4, rows - 4))
    sweep(theta, (5, rows - 5))
    for c, W in enumerate((A, B, C)):
        for k, at in ((0, 1), (1, rows - 6)):
            outs.append((W.at[pl.ds(at, 5), wide], rim_ref.at[c, pl.ds(5 * k, 5)]))
    outs = [pltpu.make_async_copy(a, b, out_sem.at[i]) for i, (a, b) in enumerate(outs)]
    for copy in outs:
        copy.start()
    pad = padded(cols)
    for d in range(GROUP):
        u_ref[d, pl.ds(0, cols)] = A[INNER[d], own]
        v_ref[d, pl.ds(0, cols)] = B[INNER[d], own]
        theta_ref[d, pl.ds(0, cols)] = C[INNER[d], own]
    for copy in outs:
        copy.wait()


def inner_rows(metric, flat, west, east_, after, cols, rows):
    lev = flat.shape[-1]
    pad = padded(cols)
    wide = window(cols)
    shapes = [(GROUP, pad, lev)] * 3 + [(3, 10, wide, lev), (3, 4, wide, lev)]
    return pl.pallas_call(
        functools.partial(inner_kernel, cols, rows),
        in_specs=[smem(), any_space(), vmem(), vmem(), any_space()],
        out_specs=[vmem()] * 3 + [any_space()] * 2,
        out_shape=[jax.ShapeDtypeStruct(s, f32) for s in shapes],
        scratch_shapes=[pltpu.VMEM((rows, LEAD + wide, lev), f32)] * 6
        + [pltpu.VMEM(flat.shape, f32), pltpu.SemaphoreType.DMA((3,)), pltpu.SemaphoreType.DMA((12,))],
        compiler_params=params(60),
        cost_estimate=cost(9),
    )(metric, flat, west, east_, after)


def edge_kernel(
    cols, rows, ids_ref, metric_ref, raw_ref, rim_ref, hn_ref, hs_ref, u_ref, v_ref, theta_ref, _, send_ref, out_ref, *scratch
):
    U, V, T, A, B, C, hold, moved, sem, move_sem, out_sem = scratch
    own = slice(LEAD, LEAD + cols)
    wide = pl.ds(LEAD - 8, window(cols))
    pad = padded(cols)
    count = HALO - 1
    loads = []
    for c, W in enumerate((U, V, T)):
        loads.append((hn_ref.at[pl.ds(count * c, count)], W.at[pl.ds(1, count), wide]))
        loads.append((hs_ref.at[pl.ds(count * c, count)], W.at[pl.ds(HALO + rows, count), wide]))
        loads.append((raw_ref.at[c, pl.ds(0, 2)], W.at[pl.ds(HALO, 2), wide]))
        loads.append((raw_ref.at[c, pl.ds(2, 2)], W.at[pl.ds(HALO + rows - 2, 2), wide]))
    loads.append((hn_ref.at[pl.ds(3 * count, 1)], T.at[pl.ds(0, 1), wide]))
    loads.append((hs_ref.at[pl.ds(3 * count, 1)], T.at[pl.ds(2 * HALO + rows - 1, 1), wide]))
    for c, W in enumerate((A, B, C)):
        loads.append((rim_ref.at[c, pl.ds(0, 5)], W.at[pl.ds(HALO + 1, 5), wide]))
        loads.append((rim_ref.at[c, pl.ds(5, 5)], W.at[pl.ds(HALO + rows - 6, 5), wide]))
    loads = [pltpu.make_async_copy(a, b, sem.at[i]) for i, (a, b) in enumerate(loads)]
    for copy in loads:
        copy.start()
    for copy in loads:
        copy.wait()
    has_north = jnp.where(ids_ref[1] > 0, 1.0, 0.0)
    has_south = jnp.where(ids_ref[2] > 0, 1.0, 0.0)

    def keep(i, x):
        return x * jnp.where(i >= HALO + rows, has_south, jnp.where(i < HALO, has_north, 1.0))

    advect, advect_theta, wind_u, wind_v, theta = stage_steps(metric_ref, HALO, U, V, T, A, B, C, keep)

    def ends(fn, lo, hi):
        sweep(fn, (HALO + lo, HALO + hi), (HALO + rows - hi, HALO + rows - lo))

    ends(advect, -3, 1)
    ends(advect_theta, -4, -3)
    ends(wind_u, -2, 1)
    ends(wind_v, -3, 2)
    ends(theta, -2, 3)
    ends(wind_u, 0, 3)
    ends(wind_v, -1, 4)
    ends(theta, 0, 5)

    @pl.when(ids_ref[3] != 0)
    def _():
        inside = pltpu.make_async_copy(
            theta_ref.at[pl.ds(1, GROUP - 2)], send_ref.at[pl.ds(1, GROUP - 2), pl.ds(3 * pad, pad)], move_sem.at[0]
        )
        inside.start()
        for d in range(GROUP):
            for c, W in enumerate((A, B, C)):
                send_ref[d, pl.ds(c * pad, cols)] = W[EDGE[d] + HALO, own]
        for d in (0, GROUP - 1):
            send_ref[d, pl.ds(3 * pad, cols)] = C[INNER[d] + HALO, own]
        inside.wait()

    @pl.when(ids_ref[3] == 0)
    def _():
        inside = [
            pltpu.make_async_copy(ref, moved.at[:, pl.ds(c * pad, pad)], move_sem.at[c])
            for c, ref in enumerate((u_ref, v_ref, theta_ref))
        ]
        for copy in inside:
            copy.start()
        for copy in inside:
            copy.wait()
        outs = [pltpu.make_async_copy(hold.at[c], out_ref.at[c], out_sem.at[c]) for c in range(3)]
        for c, W in enumerate((A, B, C)):
            for d in range(GROUP):
                hold[c, pl.ds(EDGE[d], cols, stride=rows), :] = W[EDGE[d] + HALO, own]
                if c == 2 and d in (0, GROUP - 1):
                    value = C[INNER[d] + HALO, own]
                else:
                    value = moved[d, pl.ds(c * pad, cols)]
                hold[c, pl.ds(INNER[d], cols, stride=rows), :] = value
            outs[c].start()
        for out in outs:
            out.wait()


def edge_rows(ids, metric, raw, rim, hn, hs, inner, after, cols, rows):
    lev = raw.shape[-1]
    pad = padded(cols)
    whole = (3, cols * rows, lev)
    return pl.pallas_call(
        functools.partial(edge_kernel, cols, rows),
        in_specs=[smem(), smem()] + [any_space()] * 8,
        out_specs=[vmem(), any_space()],
        out_shape=[jax.ShapeDtypeStruct((GROUP, 4 * pad, lev), f32), jax.ShapeDtypeStruct(whole, f32)],
        scratch_shapes=[pltpu.VMEM((rows + 2 * HALO, LEAD + window(cols), lev), f32)] * 6
        + [pltpu.VMEM(whole, f32), pltpu.VMEM((GROUP, 3 * pad, lev), f32)]
        + [pltpu.SemaphoreType.DMA((n,)) for n in (20, 3, 3)],
        compiler_params=params(60),
        cost_estimate=cost(8),
    )(ids, metric, raw, rim, hn, hs, *inner, after)


def offset_tables(length):
    half = length // 2
    pad = -(-half // 256) * 256
    n = np.arange(2 * pad) - pad
    tables = []
    for first in (0, 1):
        wave = np.arange(first, half + 1, 2)
        weight = np.where((wave == 0) | (wave == half), 1.0, 2.0) / length
        angle = (wave[:, None] * n[None, :]) % length * (2.0 * np.pi / length)
        tables.append((wave, (np.cos(angle) * weight[:, None]).astype(np.float32)))
    return tables


def offset_values(limits, length):
    values = []
    for wave, table in offset_tables(length):
        w = jnp.asarray(wave, f32)
        lim = limits[:, None]
        factor = jnp.where(w[None, :] <= lim, 1.0, (lim / jnp.maximum(w, 1.0)[None, :]) ** 2)
        values.append(jnp.dot(factor, jnp.asarray(table), precision=lax.Precision.HIGHEST, preferred_element_type=f32))
    return jnp.stack(values, axis=1)[:, :, None, :]


def skew(p, store):
    width = p.shape[-1]
    line = lax.broadcasted_iota(jnp.int32, (8, width), 0)
    x = jnp.broadcast_to(p, (8, width))
    for bit in range(3):
        x = jnp.where((line & (1 << bit)) != 0, pltpu.roll(x, 1 << bit, 1), x)
    for pair in range(8):
        two = [pltpu.roll(x, 8 * g, 1)[:, 128:] if g else x[:, 128:] for g in (2 * pair, 2 * pair + 1)]
        y = jnp.concatenate(two, axis=0)
        hi = y.astype(bf16)
        store(16 * pair, hi, (y - hi.astype(f32)).astype(bf16))


def skew_kernel(p_ref, hi_ref, lo_ref):
    rows, parts, _, width = p_ref.shape
    for r in range(rows):
        for e in range(parts):

            def store(at, hi, lo, r=r, e=e):
                hi_ref[r, e, at : at + 16] = hi
                lo_ref[r, e, at : at + 16] = lo

            skew(p_ref[r, e], store)


def skewed(values):
    rows, parts, _, width = values.shape
    out = jax.ShapeDtypeStruct((rows, parts, 128, width - 128), bf16)
    return pl.pallas_call(
        skew_kernel,
        in_specs=[vmem()],
        out_specs=[vmem()] * 2,
        out_shape=[out, out],
        compiler_params=params(16),
    )(values)


def filter_kernel(groups, cols, hi_ref, lo_ref, x_ref, y_ref, S, D, Y, Z):
    quarter = GROUP // 2
    size = S.shape[0]
    lev = x_ref.shape[-1]
    pad = padded(cols)
    units = [u for _, members in groups for u in members]
    S[quarter * cols :] = jnp.zeros((size - quarter * cols, S.shape[1]), f32)
    D[quarter * cols :] = jnp.zeros((size - quarter * cols, S.shape[1]), f32)
    for b in range(quarter):
        at = slice(b * cols, (b + 1) * cols)
        for i, u in enumerate(units):
            lanes = slice(i * lev, (i + 1) * lev)
            one = x_ref[b, pl.ds(u * pad, cols)]
            two = x_ref[b + quarter, pl.ds(u * pad, cols)]
            S[at, lanes] = one + two
            D[at, lanes] = one - two
    tall = size // 128
    first = 0
    for row, members in groups:
        lanes = slice(first * lev, (first + len(members)) * lev)
        first += len(members)

        def matrix(ref, e, row=row):
            starts = [(tall - 1 - b) * 128 for b in range(tall)]
            return jnp.concatenate([ref[row, e, :, st : st + size] for st in starts], axis=0)

        for e, (src, dst) in enumerate(((S, Y), (D, Z))):
            x = src[:, lanes]
            xh = x.astype(bf16)
            xl = (x - xh.astype(f32)).astype(bf16)
            mh = matrix(hi_ref, e)
            left = jnp.concatenate([mh, mh, matrix(lo_ref, e)], axis=1)
            right = jnp.concatenate([xh, xl, xh], axis=0)
            dst[:, lanes] = jnp.dot(left, right, preferred_element_type=f32)
    for b in range(quarter):
        at = slice(b * cols, (b + 1) * cols)
        for i, u in enumerate(units):
            lanes = slice(i * lev, (i + 1) * lev)
            y = Y[at, lanes]
            z = Z[at, lanes]
            y_ref[b, pl.ds(u * pad, cols)] = y + z
            y_ref[b + quarter, pl.ds(u * pad, cols)] = y - z


def filtered(groups, hi, lo, whole, cols):
    _, tall, lev = whole.shape
    count = sum(len(members) for _, members in groups)
    work = pltpu.VMEM((hi.shape[-1] - 128 * 5, count * lev), f32)
    return pl.pallas_call(
        functools.partial(filter_kernel, groups, cols),
        in_specs=[vmem()] * 3,
        out_specs=vmem(),
        out_shape=jax.ShapeDtypeStruct(whole.shape, f32),
        scratch_shapes=[work] * 4,
        compiler_params=params(32),
    )(hi, lo, whole)


def join_kernel(cols, rows, ids_ref, y_ref, m_ref, _, out_ref, held, moved, result, sem, out_sem):
    @pl.when(ids_ref[3] != 0)
    def _():
        pad = padded(cols)
        copies = [pltpu.make_async_copy(y_ref.at[:, pl.ds(u * pad, pad)], held.at[u], sem.at[u]) for u in range(4)]
        copies += [pltpu.make_async_copy(m_ref.at[:, pl.ds(u * pad, pad)], moved.at[u], sem.at[4 + u]) for u in range(2)]
        outs = [pltpu.make_async_copy(result.at[c], out_ref.at[c], out_sem.at[c]) for c in range(3)]
        for copy in copies:
            copy.start()
        for c, inner, wait in ((0, moved.at[0], 4), (1, moved.at[1], 5), (2, held.at[3], 3)):
            copies[c].wait()
            copies[wait].wait()
            for d in range(GROUP):
                result[c, pl.ds(EDGE[d], cols, stride=rows), :] = held[c, d, 0:cols]
                result[c, pl.ds(INNER[d], cols, stride=rows), :] = inner[d, 0:cols]
            outs[c].start()
        for c in range(3):
            outs[c].wait()


def joined(ids, whole, moved, other, cols, rows):
    lev = whole.shape[-1]
    pad = padded(cols)
    return pl.pallas_call(
        functools.partial(join_kernel, cols, rows),
        in_specs=[smem()] + [any_space()] * 3,
        out_specs=any_space(),
        out_shape=jax.ShapeDtypeStruct(other.shape, f32),
        scratch_shapes=[
            pltpu.VMEM((4, GROUP, pad, lev), f32),
            pltpu.VMEM((2, GROUP, pad, lev), f32),
            pltpu.VMEM(other.shape, f32),
            pltpu.SemaphoreType.DMA((6,)),
            pltpu.SemaphoreType.DMA((3,)),
        ],
        input_output_aliases={3: 0},
        compiler_params=params(16),
    )(ids, whole, moved, other)


def tie_kernel(x_ref, _, out_ref):
    pass


def tied(x, y):
    return pl.pallas_call(
        tie_kernel,
        in_specs=[any_space()] * 2,
        out_specs=any_space(),
        out_shape=jax.ShapeDtypeStruct(x.shape, x.dtype),
        input_output_aliases={0: 0},
        compiler_params=params(1),
    )(x, y)


def swapped(x):
    return lax.all_to_all(x, "lon", split_axis=0, concat_axis=0, tiled=True)


def body(state, cutoffs):
    lat_count = lax.axis_size("lat")
    lon_count = lax.axis_size("lon")
    _, cols, rows, lev = state.shape
    total_lat = rows * lat_count
    total_lon = cols * lon_count
    band = lax.axis_index("lat")
    me = lax.axis_index("lon")
    quarter = lat_count // 4
    polar = (band < quarter) | (band >= lat_count - quarter)
    ids = jnp.stack([me, band, lat_count - 1 - band, polar.astype(jnp.int32)]).astype(jnp.int32)

    up = [(i, i + 1) for i in range(lat_count - 1)]
    down = [(j, i) for i, j in up]
    right = [(i, (i + 1) % lon_count) for i in range(lon_count)]
    left = [(j, i) for i, j in right]

    flat = state.reshape(3, cols * rows, lev)
    west = lax.ppermute(state[:, cols - HALO :].reshape(3, HALO * rows, lev), "lon", right)
    east_ = lax.ppermute(state[:, :HALO].reshape(3, HALO * rows, lev), "lon", left)
    outward = [(b, b + quarter) for b in range(quarter)]
    outward += [(b, b - quarter) for b in range(lat_count - quarter, lat_count)]
    inward = [(j, i) for i, j in outward]
    near = band * rows - HALO + jnp.arange(rows + 2 * HALO, dtype=jnp.int32)
    latitude = (-90.0 + (near.astype(f32) + 0.5) * (180.0 / total_lat)) * (jnp.pi / 180.0)
    metric = 1.0 / jnp.maximum(jnp.cos(latitude), 1.0 / CAP)

    wanted = jnp.stack([edge_row(me), inner_row(me)])
    chosen = wanted[:, None] == jnp.arange(rows, dtype=jnp.int32)[None, :]
    picked = jnp.sum(jnp.where(chosen, cutoffs.astype(f32)[None, :], 0.0), axis=1)
    offsets = offset_values(picked, total_lon)
    hi, lo = skewed(offsets)
    send_north, send_south = row_sends(flat, west, east_, lo, cols, rows)
    halo_north = lax.ppermute(send_south, "lat", up)
    halo_south = lax.ppermute(send_north, "lat", down)

    u, v, theta, rim, raw = inner_rows(metric, flat, west, east_, send_north, cols, rows)
    moved_u = lax.ppermute(u, "lat", outward)
    moved_v = lax.ppermute(v, "lat", outward)
    moved_offsets = lax.ppermute(offsets[1:], "lat", outward)
    pieces, other = edge_rows(ids, metric, raw, rim, halo_north, halo_south, (u, v, theta), lo, cols, rows)

    def near_pole(pieces):
        return filtered(((0, (0, 1, 2)), (1, (3,))), hi, lo, swapped(pieces), cols)

    def elsewhere(u, v, offsets):
        moved = jnp.concatenate([u, v], axis=1)
        return swapped(filtered(((0, (0, 1)),), *skewed(offsets), swapped(moved), cols))

    pieces = lax.cond(polar, near_pole, lambda pieces: pieces, pieces)
    moved_u = tied(moved_u, pieces)
    moved = lax.cond(polar, lambda u, v, _: jnp.concatenate([u, v], axis=1), elsewhere, moved_u, moved_v, moved_offsets)
    moved = lax.ppermute(moved, "lat", inward)
    pieces = lax.cond(polar, swapped, lambda x: x, pieces)
    return joined(ids, pieces, moved, other, cols, rows).reshape(3, cols, rows, lev)


def solution(mesh):
    placed = (P(None, "lon", "lat", None), P("lat"))
    return jax.shard_map(
        body, mesh=mesh, in_specs=placed, out_specs=P(None, "lon", "lat", None), check_vma=False
    )
```

profile of v0, /device:TPU:28, one launch (start us, length us, event | category | flops | bytes accessed | tf_op | source)
XLA Modules:
  0.0 174.6 jit_solution(12009889756571190221)
XLA Ops:
  0.0 1.1 fusion.15
  1.1 1.3 collective-permute-start
  2.4 3.6 %collective-permute-start.1 = (f32[3,80,128]{2,1,0:T(8,128)S(1)}, f32[3,80,128]{2,1,0:T(8,128)S(1)}, u32[]{:S(2)}, u32[]{:S(2)}) collective-permute-start(f32[3,80,128]{2,1,0:T(8,128)S(1)} %bitcast.16), channel_id=1, source_target_pairs={{1,0},{2,1},{3,2},{4,3},{5,4},{6,5},{7,6},{0,7},{9,8},{10,9},{11,1... | collective-permute-start | bytes 368648 | tf_op jit(solution)/shard_map/ppermute | solution.py:497
  6.0 0.7 convert_element_type.14
  6.9 2.8 %fusion.2 = f32[2,1536]{1,0:T(2,128)S(1)} fusion(f32[360,1536]{1,0:T(8,128)} %constant.48.clone, f32[360]{0:T(512)} %constant.53, f32[360]{0:T(512)} %constant.47.clone, f32[2]{0:T(128)S(1)} %fusion.12), kind=kOutput, calls=%fused_computation.11 | convolution fusion | flops 13273920 | bytes 2227016 | tf_op jit(solution)/shard_map/dot_general | solution.py:320
  9.7 1.2 fusion.3
  11.0 2.8 %shard_map.64 = (bf16[2,2,128,1408]{3,2,1,0:T(8,128)(2,1)}, bf16[2,2,128,1408]{3,2,1,0:T(8,128)(2,1)S(1)}) custom-call(f32[2,2,1,1536]{3,2,1,0:T(1,128)S(1)} %broadcast_in_dim.36.p_ref), custom_call_target="tpu_custom_call" | custom-call | tf_op jit(solution)/shard_map/pallas_call | solution.py:352
  13.8 0.7 copy-done.8
  14.6 5.1 %shard_map.65 = (f32[13,200,128]{2,1,0:T(8,128)}, f32[13,200,128]{2,1,0:T(8,128)}) custom-call(f32[3,2880,128]{2,1,0:T(8,128)} %bitcast.14, f32[3,80,128]{2,1,0:T(8,128)} %copy-done.8, f32[3,80,128]{2,1,0:T(8,128)} %copy-done.9, bf16[2,2,128,1408]{3,2,1,0:T(8,128)(2,1)S(1)} %get-tuple-element.54._), custom_call_target="tpu_custom_call" | custom-call | bytes 14760000 | tf_op jit(solution)/shard_map/pallas_call | solution.py:87
  19.7 1.9 %collective-permute-start.2 = (f32[13,200,128]{2,1,0:T(8,128)}, f32[13,200,128]{2,1,0:T(8,128)S(1)}, u32[]{:S(2)}, u32[]{:S(2)}) collective-permute-start(f32[13,200,128]{2,1,0:T(8,128)} %get-tuple-element.58), channel_id=1, source_target_pairs={{0,8},{8,16},{16,24},{24,32},{32,40},{40,48},{48,56},{56,64},{64,7... | collective-permute-start | bytes 3993608 | tf_op jit(solution)/shard_map/ppermute | solution.py:511
  21.6 5.1 %collective-permute-start.3 = (f32[13,200,128]{2,1,0:T(8,128)}, f32[13,200,128]{2,1,0:T(8,128)S(1)}, u32[]{:S(2)}, u32[]{:S(2)}) collective-permute-start(f32[13,200,128]{2,1,0:T(8,128)} %get-tuple-element.55._), channel_id=1, source_target_pairs={{8,0},{16,8},{24,16},{32,24},{40,32},{48,40},{56,48},{64,56},{72,6... | collective-permute-start | bytes 3993608 | tf_op jit(solution)/shard_map/ppermute | solution.py:512
  26.8 0.6 maximum_divide_fusion.metric_ref
  27.4 11.3 %shard_map.66 = (f32[8,184,128]{2,1,0:T(8,128)}, f32[8,184,128]{2,1,0:T(8,128)}, f32[8,184,128]{2,1,0:T(8,128)}, f32[3,10,200,128]{3,2,1,0:T(8,128)}, f32[3,4,200,128]{3,2,1,0:T(8,128)}) custom-call(f32[26]{0:T(128)} %maximum_divide_fusion.metric_ref, f32[3,2880,128]{2,1,0:T(8,128)} %bitcast.15, f32[3,80,128]{2,1,0:T(8,128)} %copy-done.8, ...), custom_call_target="tpu_custom_call" | custom-call | bytes 33210000 | tf_op jit(solution)/shard_map/pallas_call | solution.py:191
  38.7 3.6 %collective-permute-start.5 = (f32[8,184,128]{2,1,0:T(8,128)}, f32[8,184,128]{2,1,0:T(8,128)}, u32[]{:S(2)}, u32[]{:S(2)}) collective-permute-start(f32[8,184,128]{2,1,0:T(8,128)} %get-tuple-element.59.u_ref), channel_id=1, source_target_pairs={{0,32},{8,40},{16,48},{24,56},{96,64},{104,72},{112,80},{120,88},{... | collective-permute-start | bytes 2261000 | tf_op jit(solution)/shard_map/ppermute | solution.py:515
  42.2 2.2 %collective-permute-start.6 = (f32[8,184,128]{2,1,0:T(8,128)}, f32[8,184,128]{2,1,0:T(8,128)}, u32[]{:S(2)}, u32[]{:S(2)}) collective-permute-start(f32[8,184,128]{2,1,0:T(8,128)} %get-tuple-element.60.v_ref), channel_id=1, source_target_pairs={{0,32},{8,40},{16,48},{24,56},{96,64},{104,72},{112,80},{120,88},{... | collective-permute-start | bytes 2261000 | tf_op jit(solution)/shard_map/ppermute | solution.py:516
  44.4 1.3 collective-permute-start.4
  45.7 0.6 pad_add_fusion.ids_ref
  46.3 4.5 %collective-permute-done.2.hn_ref = f32[13,200,128]{2,1,0:T(8,128)S(1)} collective-permute-done((f32[13,200,128]{2,1,0:T(8,128)}, f32[13,200,128]{2,1,0:T(8,128)S(1)}, u32[]{:S(2)}, u32[]{:S(2)}) %collective-permute-start.2) | collective-permute-done | bytes 1331232 | tf_op jit(solution)/shard_map/ppermute | solution.py:511
  50.9 1.1 copy-done.6
  52.4 7.4 %shard_map.67 = (f32[8,736,128]{2,1,0:T(8,128)S(1)}, f32[3,2880,128]{2,1,0:T(8,128)}) custom-call(s32[4]{0:T(128)} %pad_add_fusion.ids_ref, f32[26]{0:T(128)} %maximum_divide_fusion.metric_ref, f32[3,4,200,128]{3,2,1,0:T(8,128)} %get-tuple-element.56.raw_ref, f32[3,10,200,128]{3,2,1,0:T(8,128)} %get-tuple-element.57.rim_ref, f32[13,200,128]{2,1,0:T(8,128)} %copy-done.6, ...), custom_call_target="tpu_custom_call" | custom-call | bytes 29520000 | tf_op jit(solution)/shard_map/pallas_call | solution.py:288
  59.8 40.5 %conditional.3 = (f32[8,736,128]{2,1,0:T(8,128)S(1)}) conditional(s32[]{:T(128)} %convert_element_type.12, f32[8,736,128]{2,1,0:T(8,128)S(1)} %get-tuple-element.62, (f32[8,736,128]{2,1,0:T(8,128)S(1)}, bf16[2,2,128,1408]{3,2,1,0:T(8,128)(2,1)}, bf16[2,2,128,1408]{3,2,1,0:T(8,128)(2,1)}) %tuple.35), branch_computations={%region_1.2_spmd, %region_2.3_spmd} | conditional | bytes 17563712 | solution.py:527
  59.9 34.5 %all_to_all.16.x_ref = f32[8,736,128]{2,1,0:T(8,128)S(1)} all-to-all(f32[8,736,128]{2,1,0:T(8,128)S(1)} %get-tuple-element.35), channel_id=1, replica_groups=mesh['lat'=16,'lon'=8] {'lon'}, dimensions={0} | all-to-all | bytes 6029312 | tf_op jit(solution)/shard_map/cond/branch_1_fun/all_to_all | solution.py:475
  94.4 5.7 %branch_1_fun.1 = f32[8,736,128]{2,1,0:T(8,128)S(1)} custom-call(bf16[2,2,128,1408]{3,2,1,0:T(8,128)(2,1)S(1)} %copy-done.5, bf16[2,2,128,1408]{3,2,1,0:T(8,128)(2,1)S(1)} %copy-done.3, f32[8,736,128]{2,1,0:T(8,128)S(1)} %all_to_all.16.x_ref), custom_call_target="tpu_custom_call" | custom-call | tf_op jit(solution)/shard_map/cond/branch_1_fun/pallas_call | solution.py:409
  100.3 1.6 copy-done.1
  101.9 1.4 conditional.5
  101.9 1.4 pad_maximum_fusion.1
  103.4 1.3 collective-permute-start.7
  104.7 34.6 %conditional.4 = (f32[8,736,128]{2,1,0:T(8,128)}) conditional(s32[]{:T(128)} %convert_element_type.12, f32[8,736,128]{2,1,0:T(8,128)} %copy-done.1, f32[8,736,128]{2,1,0:T(8,128)} %copy-done.1), branch_computations={%region_3.4_spmd, %region_4.5_spmd} | conditional | bytes 12058632 | solution.py:531
  104.7 1.9 %copy.19 = f32[8,736,128]{2,1,0:T(8,128)S(1)} copy(f32[8,736,128]{2,1,0:T(8,128)} %param.3) | data formatting | bytes 6029312 | tf_op jit(solution)/shard_map/cond
  106.5 32.8 %all_to_all.17 = f32[8,736,128]{2,1,0:T(8,128)} all-to-all(f32[8,736,128]{2,1,0:T(8,128)S(1)} %copy.19), channel_id=1, replica_groups=mesh['lat'=16,'lon'=8] {'lon'}, dimensions={0} | all-to-all | bytes 6029312 | tf_op jit(solution)/shard_map/cond/branch_1_fun/all_to_all | solution.py:475
  139.3 30.0 %collective-permute-done.7.m_ref = f32[8,368,128]{2,1,0:T(8,128)S(1)} collective-permute-done((f32[8,368,128]{2,1,0:T(8,128)S(1)}, f32[8,368,128]{2,1,0:T(8,128)S(1)}, u32[]{:S(2)}, u32[]{:S(2)}) %collective-permute-start.7) | collective-permute-done | bytes 1507360 | tf_op jit(solution)/shard_map/ppermute | solution.py:530
  169.3 5.1 %shard_map.69 = f32[3,2880,128]{2,1,0:T(8,128)} custom-call(s32[4]{0:T(128)S(1)} %copy-done, f32[8,736,128]{2,1,0:T(8,128)} %get-tuple-element.74.y_ref, f32[8,368,128]{2,1,0:T(8,128)S(1)} %collective-permute-done.7.m_ref, f32[3,2880,128]{2,1,0:T(8,128)} %get-tuple-element.64._), custom_call_target="tpu_custom_call", output_to_operand_aliasing={{}: (3, {})} | custom-call | tf_op jit(solution)/shard_map/pallas_call | solution.py:442
  (35 shorter events, 0.9 us)
Async XLA Ops:
  0.0 9.7 %copy-start.10 = (f32[361]{0:T(512)S(1)}, f32[361]{0:T(512)}, u32[]{:S(2)}) copy-start(f32[361]{0:T(512)} %constant.52) | copy-start | bytes 4336
  0.0 9.7 %copy-start.4 = (f32[361,1536]{1,0:T(8,128)S(1)}, f32[361,1536]{1,0:T(8,128)}, u32[]{:S(2)}) copy-start(f32[361,1536]{1,0:T(8,128)} %constant.46.clone) | copy-start | bytes 6653956
  0.0 9.7 %copy-start.11 = (f32[361]{0:T(512)S(1)}, f32[361]{0:T(512)}, u32[]{:S(2)}) copy-start(f32[361]{0:T(512)} %constant.45.clone) | copy-start | bytes 4336
  1.1 12.7 %collective-permute-start = (f32[3,80,128]{2,1,0:T(8,128)S(1)}, f32[3,80,128]{2,1,0:T(8,128)S(1)}, u32[]{:S(2)}, u32[]{:S(2)}) collective-permute-start(f32[3,80,128]{2,1,0:T(8,128)S(1)} %bitcast.17), channel_id=1, source_target_pairs={{0,1},{1,2},{2,3},{3,4},{4,5},{5,6},{6,7},{7,0},{8,9},{9,10},{10,1... | collective-permute-start | bytes 368648 | tf_op jit(solution)/shard_map/ppermute | solution.py:496
  2.4 11.4 %collective-permute-start.1 = (f32[3,80,128]{2,1,0:T(8,128)S(1)}, f32[3,80,128]{2,1,0:T(8,128)S(1)}, u32[]{:S(2)}, u32[]{:S(2)}) collective-permute-start(f32[3,80,128]{2,1,0:T(8,128)S(1)} %bitcast.16), channel_id=1, source_target_pairs={{1,0},{2,1},{3,2},{4,3},{5,4},{6,5},{7,6},{0,7},{9,8},{10,9},{11,1... | collective-permute-start | bytes 368648 | tf_op jit(solution)/shard_map/ppermute | solution.py:497
  13.8 5.9 %copy-start.2 = (bf16[2,2,128,1408]{3,2,1,0:T(8,128)(2,1)}, bf16[2,2,128,1408]{3,2,1,0:T(8,128)(2,1)S(1)}, u32[]{:S(2)}) copy-start(bf16[2,2,128,1408]{3,2,1,0:T(8,128)(2,1)S(1)} %get-tuple-element.54._) | copy-start | bytes 4325380
  13.8 0.7 copy-start.8
  13.8 0.7 copy-start.9
  19.7 31.1 %collective-permute-start.2 = (f32[13,200,128]{2,1,0:T(8,128)}, f32[13,200,128]{2,1,0:T(8,128)S(1)}, u32[]{:S(2)}, u32[]{:S(2)}) collective-permute-start(f32[13,200,128]{2,1,0:T(8,128)} %get-tuple-element.58), channel_id=1, source_target_pairs={{0,8},{8,16},{16,24},{24,32},{32,40},{40,48},{48,56},{56,64},{64,7... | collective-permute-start | bytes 3993608 | tf_op jit(solution)/shard_map/ppermute | solution.py:511
  21.6 29.2 %collective-permute-start.3 = (f32[13,200,128]{2,1,0:T(8,128)}, f32[13,200,128]{2,1,0:T(8,128)S(1)}, u32[]{:S(2)}, u32[]{:S(2)}) collective-permute-start(f32[13,200,128]{2,1,0:T(8,128)} %get-tuple-element.55._), channel_id=1, source_target_pairs={{8,0},{16,8},{24,16},{32,24},{40,32},{48,40},{56,48},{64,56},{72,6... | collective-permute-start | bytes 3993608 | tf_op jit(solution)/shard_map/ppermute | solution.py:512
  38.7 61.6 %collective-permute-start.5 = (f32[8,184,128]{2,1,0:T(8,128)}, f32[8,184,128]{2,1,0:T(8,128)}, u32[]{:S(2)}, u32[]{:S(2)}) collective-permute-start(f32[8,184,128]{2,1,0:T(8,128)} %get-tuple-element.59.u_ref), channel_id=1, source_target_pairs={{0,32},{8,40},{16,48},{24,56},{96,64},{104,72},{112,80},{120,88},{... | collective-permute-start | bytes 2261000 | tf_op jit(solution)/shard_map/ppermute | solution.py:515
  42.2 59.7 %collective-permute-start.6 = (f32[8,184,128]{2,1,0:T(8,128)}, f32[8,184,128]{2,1,0:T(8,128)}, u32[]{:S(2)}, u32[]{:S(2)}) collective-permute-start(f32[8,184,128]{2,1,0:T(8,128)} %get-tuple-element.60.v_ref), channel_id=1, source_target_pairs={{0,32},{8,40},{16,48},{24,56},{96,64},{104,72},{112,80},{120,88},{... | collective-permute-start | bytes 2261000 | tf_op jit(solution)/shard_map/ppermute | solution.py:516
  44.4 57.5 %collective-permute-start.4 = (f32[1,2,1,1536]{3,1,2,0:T(2,128)S(1)}, f32[1,2,1,1536]{3,1,2,0:T(2,128)S(1)}, u32[]{:S(2)}, u32[]{:S(2)}) collective-permute-start(f32[1,2,1,1536]{3,1,2,0:T(2,128)S(1)} %fusion.1), channel_id=1, source_target_pairs={{0,32},{8,40},{16,48},{24,56},{96,64},{104,72},{112,80},{120,88},{... | collective-permute-start | bytes 36872 | tf_op jit(solution)/shard_map/ppermute | solution.py:517
  50.8 1.1 copy-start.6
  50.9 1.6 copy-start.7
  59.8 34.5 %copy-start.3 = (bf16[2,2,128,1408]{3,2,1,0:T(8,128)(2,1)S(1)}, bf16[2,2,128,1408]{3,2,1,0:T(8,128)(2,1)}, u32[]{:S(2)}) copy-start(bf16[2,2,128,1408]{3,2,1,0:T(8,128)(2,1)} %get-tuple-element.34.lo_ref) | copy-start | bytes 4325380 | tf_op jit(solution)/shard_map/cond
  59.9 34.5 %copy-start.5 = (bf16[2,2,128,1408]{3,2,1,0:T(8,128)(2,1)S(1)}, bf16[2,2,128,1408]{3,2,1,0:T(8,128)(2,1)}, u32[]{:S(2)}) copy-start(bf16[2,2,128,1408]{3,2,1,0:T(8,128)(2,1)} %get-tuple-element.33.hi_ref) | copy-start | bytes 4325380 | tf_op jit(solution)/shard_map/cond
  100.3 1.6 copy-start.1
  103.4 65.9 %copy-start = (s32[4]{0:T(128)S(1)}, s32[4]{0:T(128)}, u32[]{:S(2)}) copy-start(s32[4]{0:T(128)} %pad_add_fusion.ids_ref) | copy-start | bytes 52
  103.4 65.9 %collective-permute-start.7 = (f32[8,368,128]{2,1,0:T(8,128)S(1)}, f32[8,368,128]{2,1,0:T(8,128)S(1)}, u32[]{:S(2)}, u32[]{:S(2)}) collective-permute-start(f32[8,368,128]{2,1,0:T(8,128)S(1)} %get-tuple-element.75), channel_id=1, source_target_pairs={{32,0},{40,8},{48,16},{56,24},{64,96},{72,104},{80,112},{88,120},{... | collective-permute-start | bytes 4521992 | tf_op jit(solution)/shard_map/ppermute | solution.py:530
where the time goes:
time: 175 us
  blocking collectives  67.3 us (38%)
  Pallas kernels  37.4 us (21%)
  waiting for transfers between devices  34.5 us (20%)
  starting transfers between devices  20.2 us (12%)
  local copies, waits for them, and re-layouts  6.93 us (4%)
  matrix products  3.99 us (2%)
  other arithmetic  3.61 us (2%)
    all_to_all x2, blocking collectives, swapped(): return lax.all_to_all(x, 'lon', split_axis=0, concat_axis=0, tiled=True)  67.3 us
    ppermute x1, waiting for transfers between devices, body(): moved = lax.ppermute(moved, 'lat', inward)  30 us
    pallas_call x1, Pallas kernels, inner_rows(): pl.pallas_call(functools.partial(inner_kernel, cols, rows), in_specs=[sme...  11.3 us
    pallas_call x1, Pallas kernels, edge_rows(): pl.pallas_call(functools.partial(edge_kernel, cols, rows), in_specs=[smem...  7.39 us
    pallas_call x1, Pallas kernels, filtered(): pl.pallas_call(functools.partial(filter_kernel, groups, cols), in_specs=[...  5.67 us
    ppermute x1, starting transfers between devices, body(): halo_south = lax.ppermute(send_north, 'lat', down)  5.15 us
    pallas_call x1, Pallas kernels, joined(): pl.pallas_call(functools.partial(join_kernel, cols, rows), in_specs=[smem...  5.13 us
    pallas_call x1, Pallas kernels, row_sends(): pl.pallas_call(functools.partial(send_kernel, cols, rows), in_specs=[any_...  5.12 us
  transfers between devices with their start and end apart: 8, of which 2 were waited for; matrix products, arithmetic and copies ran while one was open for 5% of the time, Pallas kernels for 16%

commit v1 on v0

--- a/solution.py
+++ b/solution.py
@@ -15,6 +15,8 @@
 CAP = 2.0
 LEAD = 16
 GROUP = 8
+UNROLL = 2
+PACK = 3
 MIB = 1024 * 1024
 
 f32 = jnp.float32
@@ -61,38 +63,89 @@
     return pl.BlockSpec(memory_space=pltpu.MemorySpace.HBM)
 
 
-def send_kernel(cols, rows, x_ref, west_ref, east_ref, _, north_ref, south_ref, hold, sem):
+def split_kernel(cols, rows, x_ref, _, __, planes_ref, north_ref, south_ref, hold, P, sem, out_sem):
+    count = HALO - 1
     loads = [pltpu.make_async_copy(x_ref.at[c], hold.at[c], sem.at[c]) for c in range(3)]
     for copy in loads:
         copy.start()
-
-    def put(ref, at, c, r):
-        ref[at, pl.ds(8, cols)] = hold[c, pl.ds(r, cols, stride=rows), :]
-        ref[at, pl.ds(8 - HALO, HALO)] = west_ref[c, pl.ds(r, HALO, stride=rows), :]
-        ref[at, pl.ds(8 + cols, HALO)] = east_ref[c, pl.ds(r, HALO, stride=rows), :]
-
-    top = rows - HALO + 1
+    outs = []
     for c in range(3):
         loads[c].wait()
-        for k in range(HALO - 1):
-            put(north_ref, (HALO - 1) * c + k, c, k)
-            put(south_ref, (HALO - 1) * c + k, c, top + k)
-    put(north_ref, 3 * (HALO - 1), 2, HALO - 1)
-    put(south_ref, 3 * (HALO - 1), 2, rows - HALO)
-
-
-def row_sends(flat, west, east_, after, cols, rows):
+        for r in range(rows):
+            P[c, r, pl.ds(8, cols)] = hold[c, pl.ds(r, cols, stride=rows), :]
+        mine = [
+            (P.at[c, pl.ds(0, count)], north_ref.at[pl.ds(count * c, count)]),
+            (P.at[c, pl.ds(rows - count, count)], south_ref.at[pl.ds(count * c, count)]),
+            (P.at[c], planes_ref.at[c]),
+        ]
+        if c == 2:
+            mine.append((P.at[c, pl.ds(count, 1)], north_ref.at[pl.ds(3 * count, 1)]))
+            mine.append((P.at[c, pl.ds(rows - HALO, 1)], south_ref.at[pl.ds(3 * count, 1)]))
+        for s, d in mine:
+            outs.append(pltpu.make_async_copy(s, d, out_sem.at[len(outs)]))
+            outs[-1].start()
+    for copy in outs:
+        copy.wait()
+
+
+def split_planes(flat, after, cols, rows):
     lev = flat.shape[-1]
-    edge = jax.ShapeDtypeStruct((3 * (HALO - 1) + 1, window(cols), lev), f32)
-    return pl.pallas_call(
-        functools.partial(send_kernel, cols, rows),
-        in_specs=[any_space(), vmem(), vmem(), any_space()],
-        out_specs=[vmem()] * 2,
-        out_shape=[edge, edge],
-        scratch_shapes=[pltpu.VMEM(flat.shape, f32), pltpu.SemaphoreType.DMA((3,))],
+    wide = window(cols)
+    edge = jax.ShapeDtypeStruct((3 * (HALO - 1) + 1, wide, lev), f32)
+    planes = (3, rows, wide, lev)
+    return pl.pallas_call(
+        functools.partial(split_kernel, cols, rows),
+        in_specs=[any_space()] * 3,
+        out_specs=[any_space()] * 3,
+        out_shape=[jax.ShapeDtypeStruct(planes, f32), edge, edge],
+        scratch_shapes=[
+            pltpu.VMEM(flat.shape, f32),
+            pltpu.VMEM(planes, f32),
+            pltpu.SemaphoreType.DMA((3,)),
+            pltpu.SemaphoreType.DMA((11,)),
+        ],
         compiler_params=params(60),
-        cost_estimate=cost(4),
-    )(flat, west, east_, after)
+    )(flat, *after)
+
+
+def column_kernel(cols, rows, west_ref, east_ref, _, __, north_ref, south_ref, W, E, sem, out_sem):
+    at = (8 + cols) // 8 * 8
+    off = 8 + cols - at
+    ends = ((north_ref, 0), (south_ref, 1))
+    loads = [pltpu.make_async_copy(ref.at[:, pl.ds(at, 16)], E.at[k], sem.at[k]) for ref, k in ends]
+    for copy in loads:
+        copy.start()
+    for k, (base, last) in enumerate(((0, HALO - 1), (rows - HALO + 1, rows - HALO))):
+        planes = [(c, base + j) for c in range(3) for j in range(HALO - 1)] + [(2, last)]
+        for n, (c, r) in enumerate(planes):
+            W[k, n, pl.ds(8 - HALO, HALO)] = west_ref[c, pl.ds(r, HALO, stride=rows), :]
+        loads[k].wait()
+        for n, (c, r) in enumerate(planes):
+            E[k, n, pl.ds(off, HALO)] = east_ref[c, pl.ds(r, HALO, stride=rows), :]
+    outs = [pltpu.make_async_copy(E.at[k], ref.at[:, pl.ds(at, 16)], sem.at[k]) for ref, k in ends]
+    outs += [pltpu.make_async_copy(W.at[k], ref.at[:, pl.ds(0, 8)], out_sem.at[k]) for ref, k in ends]
+    for copy in outs:
+        copy.start()
+    for copy in outs:
+        copy.wait()
+
+
+def with_columns(west, east_, north, south, cols, rows):
+    count, _, lev = north.shape
+    return pl.pallas_call(
+        functools.partial(column_kernel, cols, rows),
+        in_specs=[vmem(), vmem(), any_space(), any_space()],
+        out_specs=[any_space()] * 2,
+        out_shape=[jax.ShapeDtypeStruct(north.shape, f32)] * 2,
+        scratch_shapes=[
+            pltpu.VMEM((2, count, 8, lev), f32),
+            pltpu.VMEM((2, count, 16, lev), f32),
+            pltpu.SemaphoreType.DMA((2,)),
+            pltpu.SemaphoreType.DMA((2,)),
+        ],
+        input_output_aliases={2: 0, 3: 1},
+        compiler_params=params(4),
+    )(west, east_, north, south)
 
 
 def east(W, r):
@@ -135,29 +188,25 @@
             fn(i)
             return carry
 
-        lax.fori_loop(lo, hi, step, 0)
+        lax.fori_loop(lo, hi, step, 0, unroll=UNROLL)
 
 
 def inner_kernel(
-    cols, rows, metric_ref, x_ref, west_ref, east_ref, _, u_ref, v_ref, theta_ref, rim_ref, raw_ref, *scratch
+    cols, rows, metric_ref, planes_ref, west_ref, east_ref, off_ref, _, u_ref, v_ref, theta_ref, rim_ref, raw_ref, *scratch
 ):
-    U, V, T, A, B, C, hold, sem, out_sem = scratch
+    U, V, T, A, B, C, sem, out_sem = scratch
     own = slice(LEAD, LEAD + cols)
     wide = pl.ds(LEAD - 8, window(cols))
-    loads = [pltpu.make_async_copy(x_ref.at[c], hold.at[c], sem.at[c]) for c in range(3)]
+    loads = [pltpu.make_async_copy(planes_ref.at[c], W.at[:, wide], sem.at[c]) for c, W in enumerate((U, V, T))]
     for copy in loads:
         copy.start()
     outs = []
     for c, W in enumerate((U, V, T)):
         loads[c].wait()
 
-        def fill(r, carry, c=c, W=W):
-            W[r, own] = hold[c, pl.ds(r, cols, stride=rows), :]
+        for r in range(rows):
             W[r, pl.ds(LEAD - HALO, HALO)] = west_ref[c, pl.ds(r, HALO, stride=rows), :]
             W[r, pl.ds(LEAD + cols, HALO)] = east_ref[c, pl.ds(r, HALO, stride=rows), :]
-            return carry
-
-        lax.fori_loop(0, rows, fill, 0)
         for k, at in ((0, 0), (1, rows - 2)):
             outs.append((W.at[pl.ds(at, 2), wide], raw_ref.at[c, pl.ds(2 * k, 2)]))
     advect, _, wind_u, wind_v, theta = stage_steps(metric_ref, 0, U, V, T, A, B, C, lambda r, x: x)
@@ -177,27 +226,28 @@
     pad = padded(cols)
     for d in range(GROUP):
         u_ref[d, pl.ds(0, cols)] = A[INNER[d], own]
+        u_ref[d, pl.ds(cols, PACK)] = off_ref[PACK * d : PACK * (d + 1)]
         v_ref[d, pl.ds(0, cols)] = B[INNER[d], own]
         theta_ref[d, pl.ds(0, cols)] = C[INNER[d], own]
     for copy in outs:
         copy.wait()
 
 
-def inner_rows(metric, flat, west, east_, after, cols, rows):
-    lev = flat.shape[-1]
+def inner_rows(metric, planes, west, east_, offsets, after, cols, rows):
+    lev = planes.shape[-1]
     pad = padded(cols)
     wide = window(cols)
     shapes = [(GROUP, pad, lev)] * 3 + [(3, 10, wide, lev), (3, 4, wide, lev)]
     return pl.pallas_call(
         functools.partial(inner_kernel, cols, rows),
-        in_specs=[smem(), any_space(), vmem(), vmem(), any_space()],
+        in_specs=[smem(), any_space(), vmem(), vmem(), vmem(), any_space()],
         out_specs=[vmem()] * 3 + [any_space()] * 2,
         out_shape=[jax.ShapeDtypeStruct(s, f32) for s in shapes],
         scratch_shapes=[pltpu.VMEM((rows, LEAD + wide, lev), f32)] * 6
-        + [pltpu.VMEM(flat.shape, f32), pltpu.SemaphoreType.DMA((3,)), pltpu.SemaphoreType.DMA((12,))],
+        + [pltpu.SemaphoreType.DMA((3,)), pltpu.SemaphoreType.DMA((12,))],
         compiler_params=params(60),
         cost_estimate=cost(9),
-    )(metric, flat, west, east_, after)
+    )(metric, planes, west, east_, offsets, after)
 
 
 def edge_kernel(
@@ -334,7 +384,32 @@
         store(16 * pair, hi, (y - hi.astype(f32)).astype(bf16))
 
 
-def skew_kernel(p_ref, hi_ref, lo_ref):
+def unpack_kernel(length, x_ref, _, hi_ref, lo_ref):
+    cols = length // GROUP
+    lines = [x_ref[d, cols + j : cols + j + 1] for d in range(GROUP) for j in range(PACK)]
+    half = len(lines) // 2
+    for e in range(2):
+
+        def store(at, hi, lo, e=e):
+            hi_ref[0, e, at : at + 16] = hi
+            lo_ref[0, e, at : at + 16] = lo
+
+        skew(jnp.concatenate(lines[e * half : (e + 1) * half], axis=1), store)
+
+
+def unpacked(x, length, after):
+    width = GROUP * PACK * x.shape[-1] // 2
+    out = jax.ShapeDtypeStruct((1, 2, 128, width - 128), bf16)
+    return pl.pallas_call(
+        functools.partial(unpack_kernel, length),
+        in_specs=[vmem(), any_space()],
+        out_specs=[vmem()] * 2,
+        out_shape=[out, out],
+        compiler_params=params(16),
+    )(x, after)
+
+
+def skew_kernel(p_ref, _, hi_ref, lo_ref):
     rows, parts, _, width = p_ref.shape
     for r in range(rows):
         for e in range(parts):
@@ -346,19 +421,19 @@
             skew(p_ref[r, e], store)
 
 
-def skewed(values):
+def skewed(values, after):
     rows, parts, _, width = values.shape
     out = jax.ShapeDtypeStruct((rows, parts, 128, width - 128), bf16)
     return pl.pallas_call(
         skew_kernel,
-        in_specs=[vmem()],
+        in_specs=[vmem(), any_space()],
         out_specs=[vmem()] * 2,
         out_shape=[out, out],
         compiler_params=params(16),
-    )(values)
-
-
-def filter_kernel(groups, cols, hi_ref, lo_ref, x_ref, y_ref, S, D, Y, Z):
+    )(values, after)
+
+
+def filter_kernel(groups, cols, hi_ref, lo_ref, x_ref, _, y_ref, S, D, Y, Z):
     quarter = GROUP // 2
     size = S.shape[0]
     lev = x_ref.shape[-1]
@@ -402,26 +477,26 @@
             y_ref[b + quarter, pl.ds(u * pad, cols)] = y - z
 
 
-def filtered(groups, hi, lo, whole, cols):
+def filtered(groups, hi, lo, whole, after, cols):
     _, tall, lev = whole.shape
     count = sum(len(members) for _, members in groups)
     work = pltpu.VMEM((hi.shape[-1] - 128 * 5, count * lev), f32)
     return pl.pallas_call(
         functools.partial(filter_kernel, groups, cols),
-        in_specs=[vmem()] * 3,
+        in_specs=[vmem()] * 3 + [any_space()],
         out_specs=vmem(),
         out_shape=jax.ShapeDtypeStruct(whole.shape, f32),
         scratch_shapes=[work] * 4,
-        compiler_params=params(32),
-    )(hi, lo, whole)
-
-
-def join_kernel(cols, rows, ids_ref, y_ref, m_ref, _, out_ref, held, moved, result, sem, out_sem):
+        compiler_params=params(28),
+    )(hi, lo, whole, after)
+
+
+def join_kernel(cols, rows, ids_ref, y_ref, u_ref, v_ref, _, out_ref, held, moved, result, sem, out_sem):
     @pl.when(ids_ref[3] != 0)
     def _():
         pad = padded(cols)
         copies = [pltpu.make_async_copy(y_ref.at[:, pl.ds(u * pad, pad)], held.at[u], sem.at[u]) for u in range(4)]
-        copies += [pltpu.make_async_copy(m_ref.at[:, pl.ds(u * pad, pad)], moved.at[u], sem.at[4 + u]) for u in range(2)]
+        copies += [pltpu.make_async_copy(ref, moved.at[u], sem.at[4 + u]) for u, ref in enumerate((u_ref, v_ref))]
         outs = [pltpu.make_async_copy(result.at[c], out_ref.at[c], out_sem.at[c]) for c in range(3)]
         for copy in copies:
             copy.start()
@@ -436,12 +511,12 @@
             outs[c].wait()
 
 
-def joined(ids, whole, moved, other, cols, rows):
+def joined(ids, whole, moved_u, moved_v, other, cols, rows):
     lev = whole.shape[-1]
     pad = padded(cols)
     return pl.pallas_call(
         functools.partial(join_kernel, cols, rows),
-        in_specs=[smem()] + [any_space()] * 3,
+        in_specs=[smem()] + [any_space()] * 4,
         out_specs=any_space(),
         out_shape=jax.ShapeDtypeStruct(other.shape, f32),
         scratch_shapes=[
@@ -451,9 +526,9 @@
             pltpu.SemaphoreType.DMA((6,)),
             pltpu.SemaphoreType.DMA((3,)),
         ],
-        input_output_aliases={3: 0},
+        input_output_aliases={4: 0},
         compiler_params=params(16),
-    )(ids, whole, moved, other)
+    )(ids, whole, moved_u, moved_v, other)
 
 
 def tie_kernel(x_ref, _, out_ref):
@@ -469,6 +544,19 @@
         input_output_aliases={0: 0},
         compiler_params=params(1),
     )(x, y)
+
+
+def hollow_kernel(out_ref):
+    pass
+
+
+def hollow(x):
+    return pl.pallas_call(
+        hollow_kernel,
+        out_specs=any_space(),
+        out_shape=jax.ShapeDtypeStruct(x.shape, x.dtype),
+        compiler_params=params(1),
+    )()
 
 
 def swapped(x):
@@ -493,8 +581,10 @@
     left = [(j, i) for i, j in right]
 
     flat = state.reshape(3, cols * rows, lev)
-    west = lax.ppermute(state[:, cols - HALO :].reshape(3, HALO * rows, lev), "lon", right)
-    east_ = lax.ppermute(state[:, :HALO].reshape(3, HALO * rows, lev), "lon", left)
+    last = state[:, cols - HALO :].reshape(3, HALO * rows, lev)
+    first = state[:, :HALO].reshape(3, HALO * rows, lev)
+    west = lax.ppermute(last, "lon", right)
+    east_ = lax.ppermute(first, "lon", left)
     outward = [(b, b + quarter) for b in range(quarter)]
     outward += [(b, b - quarter) for b in range(lat_count - quarter, lat_count)]
     inward = [(j, i) for i, j in outward]
@@ -506,30 +596,39 @@
     chosen = wanted[:, None] == jnp.arange(rows, dtype=jnp.int32)[None, :]
     picked = jnp.sum(jnp.where(chosen, cutoffs.astype(f32)[None, :], 0.0), axis=1)
     offsets = offset_values(picked, total_lon)
-    hi, lo = skewed(offsets)
-    send_north, send_south = row_sends(flat, west, east_, lo, cols, rows)
+    token = jnp.zeros((8, lev), f32)
+    packed = offsets[1].reshape(GROUP * PACK, lev)
+    hi, lo = skewed(offsets, token)
+    planes, own_north, own_south = split_planes(flat, (last, first), cols, rows)
+    send_north, send_south = with_columns(west, east_, own_north, own_south, cols, rows)
     halo_north = lax.ppermute(send_south, "lat", up)
     halo_south = lax.ppermute(send_north, "lat", down)
 
-    u, v, theta, rim, raw = inner_rows(metric, flat, west, east_, send_north, cols, rows)
+    u, v, theta, rim, raw = inner_rows(metric, planes, west, east_, packed, send_north, cols, rows)
     moved_u = lax.ppermute(u, "lat", outward)
     moved_v = lax.ppermute(v, "lat", outward)
-    moved_offsets = lax.ppermute(offsets[1:], "lat", outward)
     pieces, other = edge_rows(ids, metric, raw, rim, halo_north, halo_south, (u, v, theta), lo, cols, rows)
 
-    def near_pole(pieces):
-        return filtered(((0, (0, 1, 2)), (1, (3,))), hi, lo, swapped(pieces), cols)
-
-    def elsewhere(u, v, offsets):
-        moved = jnp.concatenate([u, v], axis=1)
-        return swapped(filtered(((0, (0, 1)),), *skewed(offsets), swapped(moved), cols))
-
-    pieces = lax.cond(polar, near_pole, lambda pieces: pieces, pieces)
-    moved_u = tied(moved_u, pieces)
-    moved = lax.cond(polar, lambda u, v, _: jnp.concatenate([u, v], axis=1), elsewhere, moved_u, moved_v, moved_offsets)
-    moved = lax.ppermute(moved, "lat", inward)
-    pieces = lax.cond(polar, swapped, lambda x: x, pieces)
-    return joined(ids, pieces, moved, other, cols, rows).reshape(3, cols, rows, lev)
+    def elsewhere(x, first, after):
+        hi, lo = unpacked(first, total_lon, after)
+        return swapped(filtered(((0, (0,)),), hi, lo, swapped(x), after, cols))
+
+    def idle(x, *_):
+        return hollow(x)
+
+    def near_pole(x, after):
+        return swapped(filtered(((0, (0, 1, 2)), (1, (3,))), hi, lo, x, after, cols))
+
+    def same(x, *_):
+        return x
+
+    whole = lax.cond(polar, swapped, same, pieces)
+    back_u = lax.cond(polar, idle, elsewhere, moved_u, moved_u, tied(token, whole))
+    moved_back_u = lax.ppermute(back_u, "lat", inward)
+    back_v = lax.cond(polar, idle, elsewhere, moved_v, moved_u, tied(token, whole))
+    moved_back_v = lax.ppermute(back_v, "lat", inward)
+    pieces = lax.cond(polar, near_pole, same, whole, tied(token, back_v))
+    return joined(ids, pieces, moved_back_u, moved_back_v, other, cols, rows).reshape(3, cols, rows, lev)
 
 
 def solution(mesh):

time: 175 us -> 157 us (0.90)
  the two profiles are of different devices: /device:TPU:28 before, /device:TPU:24 now
where the time goes in v1:
time: 157 us; the launch traced here: 156 us
  blocking collectives  77.1 us (49%)
  Pallas kernels  40.6 us (26%)
  starting transfers between devices  19 us (12%)
  waiting for transfers between devices  7.65 us (5%)
  local copies, waits for them, and re-layouts  4.55 us (3%)
  matrix products  3.99 us (3%)
  other arithmetic  2.26 us (1%)
    all_to_all x2, blocking collectives, swapped(): return lax.all_to_all(x, 'lon', split_axis=0, concat_axis=0, tiled=True)  77.1 us
    pallas_call x1, Pallas kernels, inner_rows(): pl.pallas_call(functools.partial(inner_kernel, cols, rows), in_specs=[sme...  9.5 us
    pallas_call x1, Pallas kernels, filtered(): pl.pallas_call(functools.partial(filter_kernel, groups, cols), in_specs=[...  8.4 us
    pallas_call x1, Pallas kernels, edge_rows(): pl.pallas_call(functools.partial(edge_kernel, cols, rows), in_specs=[smem...  7.14 us
    pallas_call x1, Pallas kernels, joined(): pl.pallas_call(functools.partial(join_kernel, cols, rows), in_specs=[smem...  5.13 us
    pallas_call x1, Pallas kernels, split_planes(): pl.pallas_call(functools.partial(split_kernel, cols, rows), in_specs=[any...  5.11 us
    ppermute x1, waiting for transfers between devices, body(): halo_south = lax.ppermute(send_north, 'lat', down)  4.35 us
    dot_general x2, matrix products, offset_values(): jnp.dot(factor, jnp.asarray(table), precision=lax.Precision.HIGHEST, pref...  3.99 us
  transfers between devices with their start and end apart: 8, of which 2 were waited for; matrix products, arithmetic and copies ran while one was open for 5% of the time, Pallas kernels for 22%

profile of v1, /device:TPU:24, one launch (start us, length us, event | category | flops | bytes accessed | tf_op | source)
XLA Modules:
  0.0 155.6 jit_solution(14904836127236953746)
XLA Ops:
  0.0 1.0 fusion.14
  1.0 1.6 %collective-permute-start = (f32[3,80,128]{2,1,0:T(8,128)S(1)}, f32[3,80,128]{2,1,0:T(8,128)S(1)}, u32[]{:S(2)}, u32[]{:S(2)}) collective-permute-start(f32[3,80,128]{2,1,0:T(8,128)S(1)} %bitcast.15), channel_id=1, source_target_pairs={{0,1},{1,2},{2,3},{3,4},{4,5},{5,6},{6,7},{7,0},{8,9},{9,10},{10,1... | collective-permute-start | bytes 368648 | tf_op jit(solution)/shard_map/ppermute | solution.py:586
  2.6 3.6 %collective-permute-start.1 = (f32[3,80,128]{2,1,0:T(8,128)S(1)}, f32[3,80,128]{2,1,0:T(8,128)S(1)}, u32[]{:S(2)}, u32[]{:S(2)}) collective-permute-start(f32[3,80,128]{2,1,0:T(8,128)S(1)} %bitcast.13), channel_id=1, source_target_pairs={{1,0},{2,1},{3,2},{4,3},{5,4},{6,5},{7,6},{0,7},{9,8},{10,9},{11,1... | collective-permute-start | bytes 368648 | tf_op jit(solution)/shard_map/ppermute | solution.py:587
  6.1 0.7 convert_element_type.15
  6.9 0.2 fusion.11
  7.0 2.8 %fusion.2 = f32[2,1536]{1,0:T(2,128)S(1)} fusion(f32[361,1536]{1,0:T(8,128)} %constant.47.clone, f32[361]{0:T(512)} %constant.53, f32[361]{0:T(512)} %constant.46.clone, f32[2]{0:T(128)S(1)} %fusion.11), kind=kOutput, calls=%fused_computation.9 | convolution fusion | flops 13310792 | bytes 2233168 | tf_op jit(solution)/shard_map/dot_general | solution.py:370
  9.9 5.1 %shard_map.64 = (f32[3,16,200,128]{3,2,1,0:T(8,128)}, f32[13,200,128]{2,1,0:T(8,128)}, f32[13,200,128]{2,1,0:T(8,128)}) custom-call(f32[3,2880,128]{2,1,0:T(8,128)} %bitcast.12, f32[3,80,128]{2,1,0:T(8,128)} %bitcast.16, f32[3,80,128]{2,1,0:T(8,128)} %bitcast.14), custom_call_target="tpu_custom_call" | custom-call | tf_op jit(solution)/shard_map/pallas_call | solution.py:96
  15.1 1.9 %shard_map.65 = (f32[13,200,128]{2,1,0:T(8,128)}, f32[13,200,128]{2,1,0:T(8,128)}) custom-call(f32[3,80,128]{2,1,0:T(8,128)S(1)} %collective-permute-done.west_ref, f32[3,80,128]{2,1,0:T(8,128)S(1)} %collective-permute-done.1.east_ref, f32[13,200,128]{2,1,0:T(8,128)} %get-tuple-element.66._, ...), custom_call_target="tpu_custom_call", output_to_operand_aliasing={{0}: (2, {}), {1}: (3, {})} | custom-call | tf_op jit(solution)/shard_map/pallas_call | solution.py:135
  17.0 4.0 %collective-permute-start.3 = (f32[13,200,128]{2,1,0:T(8,128)}, f32[13,200,128]{2,1,0:T(8,128)S(1)}, u32[]{:S(2)}, u32[]{:S(2)}) collective-permute-start(f32[13,200,128]{2,1,0:T(8,128)} %get-tuple-element.68._), channel_id=1, source_target_pairs={{8,0},{16,8},{24,16},{32,24},{40,32},{48,40},{56,48},{64,56},{72,6... | collective-permute-start | bytes 3993608 | tf_op jit(solution)/shard_map/ppermute | solution.py:605
  21.0 1.9 %collective-permute-start.2 = (f32[13,200,128]{2,1,0:T(8,128)}, f32[13,200,128]{2,1,0:T(8,128)S(1)}, u32[]{:S(2)}, u32[]{:S(2)}) collective-permute-start(f32[13,200,128]{2,1,0:T(8,128)} %get-tuple-element.71), channel_id=1, source_target_pairs={{0,8},{8,16},{16,24},{24,32},{32,40},{40,48},{48,56},{56,64},{64,7... | collective-permute-start | bytes 3993608 | tf_op jit(solution)/shard_map/ppermute | solution.py:604
  22.9 1.2 fusion.1
  24.1 0.6 reshape_squeeze.3.off_ref
  24.8 0.6 maximum_divide_fusion.metric_ref
  25.4 9.5 %shard_map.66 = (f32[8,184,128]{2,1,0:T(8,128)}, f32[8,184,128]{2,1,0:T(8,128)}, f32[8,184,128]{2,1,0:T(8,128)}, f32[3,10,200,128]{3,2,1,0:T(8,128)}, f32[3,4,200,128]{3,2,1,0:T(8,128)}) custom-call(f32[26]{0:T(128)} %maximum_divide_fusion.metric_ref, f32[3,16,200,128]{3,2,1,0:T(8,128)} %get-tuple-element.65.planes_ref, f32[3,80,128]{2,1,0:T(8,128)} %copy-done, ...), custom_call_target="tpu_custom_call" | custom-call | bytes 33210000 | tf_op jit(solution)/shard_map/pallas_call | solution.py:241
  34.9 3.3 %collective-permute-start.4 = (f32[8,184,128]{2,1,0:T(8,128)}, f32[8,184,128]{2,1,0:T(8,128)}, u32[]{:S(2)}, u32[]{:S(2)}) collective-permute-start(f32[8,184,128]{2,1,0:T(8,128)} %get-tuple-element.72.u_ref), channel_id=1, source_target_pairs={{0,32},{8,40},{16,48},{24,56},{96,64},{104,72},{112,80},{120,88},{... | collective-permute-start | bytes 2261000 | tf_op jit(solution)/shard_map/ppermute | solution.py:608
  38.2 2.2 %collective-permute-start.5 = (f32[8,184,128]{2,1,0:T(8,128)}, f32[8,184,128]{2,1,0:T(8,128)}, u32[]{:S(2)}, u32[]{:S(2)}) collective-permute-start(f32[8,184,128]{2,1,0:T(8,128)} %get-tuple-element.73.v_ref), channel_id=1, source_target_pairs={{0,32},{8,40},{16,48},{24,56},{96,64},{104,72},{112,80},{120,88},{... | collective-permute-start | bytes 2261000 | tf_op jit(solution)/shard_map/ppermute | solution.py:609
  40.4 3.4 %shard_map.67 = (bf16[2,2,128,1408]{3,2,1,0:T(8,128)(2,1)}, bf16[2,2,128,1408]{3,2,1,0:T(8,128)(2,1)}) custom-call(f32[2,2,1,1536]{3,2,1,0:T(1,128)S(1)} %broadcast_in_dim.39.p_ref, f32[8,128]{1,0:T(8,128)S(1)} %broadcast_in_dim.40._.x_ref), custom_call_target="tpu_custom_call" | custom-call | tf_op jit(solution)/shard_map/pallas_call | solution.py:427
  43.8 0.7 pad_add_fusion.ids_ref
  44.5 4.3 %collective-permute-done.3.hs_ref = f32[13,200,128]{2,1,0:T(8,128)S(1)} collective-permute-done((f32[13,200,128]{2,1,0:T(8,128)}, f32[13,200,128]{2,1,0:T(8,128)S(1)}, u32[]{:S(2)}, u32[]{:S(2)}) %collective-permute-start.3) | collective-permute-done | bytes 1331232 | tf_op jit(solution)/shard_map/ppermute | solution.py:605
  48.8 3.3 %collective-permute-done.2.hn_ref = f32[13,200,128]{2,1,0:T(8,128)S(1)} collective-permute-done((f32[13,200,128]{2,1,0:T(8,128)}, f32[13,200,128]{2,1,0:T(8,128)S(1)}, u32[]{:S(2)}, u32[]{:S(2)}) %collective-permute-start.2) | collective-permute-done | bytes 1331232 | tf_op jit(solution)/shard_map/ppermute | solution.py:604
  52.1 1.1 copy-done.6
  53.2 7.1 %shard_map.68 = (f32[8,736,128]{2,1,0:T(8,128)S(1)}, f32[3,2880,128]{2,1,0:T(8,128)}) custom-call(s32[4]{0:T(128)} %pad_add_fusion.ids_ref, f32[26]{0:T(128)} %maximum_divide_fusion.metric_ref, f32[3,4,200,128]{3,2,1,0:T(8,128)} %get-tuple-element.69.raw_ref, f32[3,10,200,128]{3,2,1,0:T(8,128)} %get-tuple-element.70.rim_ref, f32[13,200,128]{2,1,0:T(8,128)} %copy-done.6, ...), custom_call_target="tpu_custom_call" | custom-call | bytes 29520000 | tf_op jit(solution)/shard_map/pallas_call | solution.py:338
  60.3 39.5 %conditional.4 = (f32[8,736,128]{2,1,0:T(8,128)S(1)}) conditional(s32[]{:T(128)} %convert_element_type.6, f32[8,736,128]{2,1,0:T(8,128)S(1)} %get-tuple-element.76, f32[8,736,128]{2,1,0:T(8,128)S(1)} %get-tuple-element.76), branch_computations={%region_1.2_spmd, %region_2.3_spmd} | conditional | bytes 12058632 | solution.py:625
  60.3 0.2 copy.25
  60.5 39.2 %all_to_all.24 = f32[8,736,128]{2,1,0:T(8,128)S(1)} all-to-all(f32[8,736,128]{2,1,0:T(8,128)S(1)} %copy.25), channel_id=1, replica_groups=mesh['lat'=16,'lon'=8] {'lon'}, dimensions={0} | all-to-all | bytes 6029312 | tf_op jit(solution)/shard_map/cond/branch_1_fun/all_to_all | solution.py:563
  99.8 1.6 %copy-done.3 = f32[8,736,128]{2,1,0:T(8,128)} copy-done((f32[8,736,128]{2,1,0:T(8,128)}, f32[8,736,128]{2,1,0:T(8,128)S(1)}, u32[]{:S(2)}) %copy-start.3) | copy-done | bytes 3014680
  101.4 1.3 collective-permute-start.6
  102.7 1.3 collective-permute-start.7
  104.0 46.3 %conditional.6 = (f32[8,736,128]{2,1,0:T(8,128)}) conditional(s32[]{:T(128)} %convert_element_type.6, f32[8,736,128]{2,1,0:T(8,128)} %copy-done.3, (bf16[2,2,128,1408]{3,2,1,0:T(8,128)(2,1)}, bf16[2,2,128,1408]{3,2,1,0:T(8,128)(2,1)}, f32[8,736,128]{2,1,0:T(8,128)}, f32[8,128]{1,0:T(8,128)S(1)}) %tuple.43), branch_computations={%region_5.6_spmd, %region_6.7_spmd} | conditional | bytes 6029320 | solution.py:630
  104.0 8.4 %branch_1_fun.4 = f32[8,736,128]{2,1,0:T(8,128)S(1)} custom-call(bf16[2,2,128,1408]{3,2,1,0:T(8,128)(2,1)} %get-tuple-element.43.hi_ref, bf16[2,2,128,1408]{3,2,1,0:T(8,128)(2,1)} %get-tuple-element.44.lo_ref, f32[8,736,128]{2,1,0:T(8,128)} %get-tuple-element.45.x_ref, f32[8,128]{1,0:T(8,128)S(1)} %get-tuple-element.46._), custom_call_target="tpu_custom_call" | custom-call | tf_op jit(solution)/shard_map/cond/branch_1_fun/pallas_call | solution.py:484
  112.5 37.9 %all_to_all.26 = f32[8,736,128]{2,1,0:T(8,128)} all-to-all(f32[8,736,128]{2,1,0:T(8,128)S(1)} %branch_1_fun.4), channel_id=1, replica_groups=mesh['lat'=16,'lon'=8] {'lon'}, dimensions={0} | all-to-all | bytes 6029312 | tf_op jit(solution)/shard_map/cond/branch_1_fun/all_to_all | solution.py:563
  150.3 5.1 %shard_map.71 = f32[3,2880,128]{2,1,0:T(8,128)} custom-call(s32[4]{0:T(128)S(1)} %copy-done.2, f32[8,736,128]{2,1,0:T(8,128)} %get-tuple-element.83.y_ref, f32[8,184,128]{2,1,0:T(8,128)S(1)} %collective-permute-done.6.u_ref, f32[8,184,128]{2,1,0:T(8,128)S(1)} %collective-permute-done.7.v_ref, ...), custom_call_target="tpu_custom_call", output_to_operand_aliasing={{}: (4, {})} | custom-call | tf_op jit(solution)/shard_map/pallas_call | solution.py:517
  (40 shorter events, 0.3 us)
Async XLA Ops:
  1.0 8.9 %copy-start.7 = (f32[3,5,16,128]{3,2,1,0:T(8,128)}, f32[3,5,16,128]{3,2,1,0:T(8,128)S(1)}, u32[]{:S(2)}) copy-start(f32[3,5,16,128]{3,2,1,0:T(8,128)S(1)} %get-tuple-element.79) | copy-start | bytes 368644
  1.0 8.9 %copy-start.8 = (f32[3,5,16,128]{3,2,1,0:T(8,128)}, f32[3,5,16,128]{3,2,1,0:T(8,128)S(1)}, u32[]{:S(2)}) copy-start(f32[3,5,16,128]{3,2,1,0:T(8,128)S(1)} %get-tuple-element.80) | copy-start | bytes 368644
  1.0 14.1 %collective-permute-start = (f32[3,80,128]{2,1,0:T(8,128)S(1)}, f32[3,80,128]{2,1,0:T(8,128)S(1)}, u32[]{:S(2)}, u32[]{:S(2)}) collective-permute-start(f32[3,80,128]{2,1,0:T(8,128)S(1)} %bitcast.15), channel_id=1, source_target_pairs={{0,1},{1,2},{2,3},{3,4},{4,5},{5,6},{6,7},{7,0},{8,9},{9,10},{10,1... | collective-permute-start | bytes 368648 | tf_op jit(solution)/shard_map/ppermute | solution.py:586
  2.6 12.5 %collective-permute-start.1 = (f32[3,80,128]{2,1,0:T(8,128)S(1)}, f32[3,80,128]{2,1,0:T(8,128)S(1)}, u32[]{:S(2)}, u32[]{:S(2)}) collective-permute-start(f32[3,80,128]{2,1,0:T(8,128)S(1)} %bitcast.13), channel_id=1, source_target_pairs={{1,0},{2,1},{3,2},{4,3},{5,4},{6,5},{7,6},{0,7},{9,8},{10,9},{11,1... | collective-permute-start | bytes 368648 | tf_op jit(solution)/shard_map/ppermute | solution.py:587
  15.0 7.9 %copy-start.4 = (f32[360,1536]{1,0:T(8,128)S(1)}, f32[360,1536]{1,0:T(8,128)}, u32[]{:S(2)}) copy-start(f32[360,1536]{1,0:T(8,128)} %constant.49.clone) | copy-start | bytes 6635524
  15.0 7.9 %copy-start.9 = (f32[360]{0:T(512)S(1)}, f32[360]{0:T(512)}, u32[]{:S(2)}) copy-start(f32[360]{0:T(512)} %constant.48.clone) | copy-start | bytes 4324
  15.1 7.9 %copy-start.10 = (f32[360]{0:T(512)S(1)}, f32[360]{0:T(512)}, u32[]{:S(2)}) copy-start(f32[360]{0:T(512)} %constant.54) | copy-start | bytes 4324
  15.1 9.0 %copy-start = (f32[3,80,128]{2,1,0:T(8,128)}, f32[3,80,128]{2,1,0:T(8,128)S(1)}, u32[]{:S(2)}) copy-start(f32[3,80,128]{2,1,0:T(8,128)S(1)} %collective-permute-done.west_ref) | copy-start | bytes 368644
  15.1 9.0 %copy-start.1 = (f32[3,80,128]{2,1,0:T(8,128)}, f32[3,80,128]{2,1,0:T(8,128)S(1)}, u32[]{:S(2)}) copy-start(f32[3,80,128]{2,1,0:T(8,128)S(1)} %collective-permute-done.1.east_ref) | copy-start | bytes 368644
  17.0 31.8 %collective-permute-start.3 = (f32[13,200,128]{2,1,0:T(8,128)}, f32[13,200,128]{2,1,0:T(8,128)S(1)}, u32[]{:S(2)}, u32[]{:S(2)}) collective-permute-start(f32[13,200,128]{2,1,0:T(8,128)} %get-tuple-element.68._), channel_id=1, source_target_pairs={{8,0},{16,8},{24,16},{32,24},{40,32},{48,40},{56,48},{64,56},{72,6... | collective-permute-start | bytes 3993608 | tf_op jit(solution)/shard_map/ppermute | solution.py:605
  21.0 31.1 %collective-permute-start.2 = (f32[13,200,128]{2,1,0:T(8,128)}, f32[13,200,128]{2,1,0:T(8,128)S(1)}, u32[]{:S(2)}, u32[]{:S(2)}) collective-permute-start(f32[13,200,128]{2,1,0:T(8,128)} %get-tuple-element.71), channel_id=1, source_target_pairs={{0,8},{8,16},{16,24},{24,32},{32,40},{40,48},{48,56},{56,64},{64,7... | collective-permute-start | bytes 3993608 | tf_op jit(solution)/shard_map/ppermute | solution.py:604
  34.9 64.9 %collective-permute-start.4 = (f32[8,184,128]{2,1,0:T(8,128)}, f32[8,184,128]{2,1,0:T(8,128)}, u32[]{:S(2)}, u32[]{:S(2)}) collective-permute-start(f32[8,184,128]{2,1,0:T(8,128)} %get-tuple-element.72.u_ref), channel_id=1, source_target_pairs={{0,32},{8,40},{16,48},{24,56},{96,64},{104,72},{112,80},{120,88},{... | collective-permute-start | bytes 2261000 | tf_op jit(solution)/shard_map/ppermute | solution.py:608
  38.2 64.5 %collective-permute-start.5 = (f32[8,184,128]{2,1,0:T(8,128)}, f32[8,184,128]{2,1,0:T(8,128)}, u32[]{:S(2)}, u32[]{:S(2)}) collective-permute-start(f32[8,184,128]{2,1,0:T(8,128)} %get-tuple-element.73.v_ref), channel_id=1, source_target_pairs={{0,32},{8,40},{16,48},{24,56},{96,64},{104,72},{112,80},{120,88},{... | collective-permute-start | bytes 2261000 | tf_op jit(solution)/shard_map/ppermute | solution.py:609
  48.8 3.3 %copy-start.5 = (f32[13,200,128]{2,1,0:T(8,128)}, f32[13,200,128]{2,1,0:T(8,128)S(1)}, u32[]{:S(2)}) copy-start(f32[13,200,128]{2,1,0:T(8,128)S(1)} %collective-permute-done.3.hs_ref) | copy-start | bytes 3993604
  52.1 1.1 copy-start.6
  99.8 1.6 %copy-start.3 = (f32[8,736,128]{2,1,0:T(8,128)}, f32[8,736,128]{2,1,0:T(8,128)S(1)}, u32[]{:S(2)}) copy-start(f32[8,736,128]{2,1,0:T(8,128)S(1)} %get-tuple-element.81._) | copy-start | bytes 9043972
  101.4 49.0 %collective-permute-start.6 = (f32[8,184,128]{2,1,0:T(8,128)}, f32[8,184,128]{2,1,0:T(8,128)S(1)}, u32[]{:S(2)}, u32[]{:S(2)}) collective-permute-start(f32[8,184,128]{2,1,0:T(8,128)} %get-tuple-element.84), channel_id=1, source_target_pairs={{32,0},{40,8},{48,16},{56,24},{64,96},{72,104},{80,112},{88,120},{... | collective-permute-start | bytes 2261000 | tf_op jit(solution)/shard_map/ppermute | solution.py:627
  102.7 47.6 %collective-permute-start.7 = (f32[8,184,128]{2,1,0:T(8,128)S(1)}, f32[8,184,128]{2,1,0:T(8,128)S(1)}, u32[]{:S(2)}, u32[]{:S(2)}) collective-permute-start(f32[8,184,128]{2,1,0:T(8,128)S(1)} %get-tuple-element.82._), channel_id=1, source_target_pairs={{32,0},{40,8},{48,16},{56,24},{64,96},{72,104},{80,112},{88,120},{... | collective-permute-start | bytes 2261000 | tf_op jit(solution)/shard_map/ppermute | solution.py:629
  104.0 46.3 %copy-start.2 = (s32[4]{0:T(128)S(1)}, s32[4]{0:T(128)}, u32[]{:S(2)}) copy-start(s32[4]{0:T(128)} %pad_add_fusion.ids_ref) | copy-start | bytes 52

commit v2 on v1

--- a/solution.py
+++ b/solution.py
@@ -250,10 +250,16 @@
     )(metric, planes, west, east_, offsets, after)
 
 
-def edge_kernel(
-    cols, rows, ids_ref, metric_ref, raw_ref, rim_ref, hn_ref, hs_ref, u_ref, v_ref, theta_ref, _, send_ref, out_ref, *scratch
+def edge_kernel(cols, rows, near_pole, ids_ref, *refs):
+    @pl.when((ids_ref[3] != 0) if near_pole else (ids_ref[3] == 0))
+    def _():
+        edge_steps(cols, rows, near_pole, ids_ref, *refs)
+
+
+def edge_steps(
+    cols, rows, near_pole, ids_ref, metric_ref, raw_ref, rim_ref, hn_ref, hs_ref, u_ref, v_ref, theta_ref, _, out_ref, *scratch
 ):
-    U, V, T, A, B, C, hold, moved, sem, move_sem, out_sem = scratch
+    U, V, T, A, B, C, sem, move_sem, *more = scratch
     own = slice(LEAD, LEAD + cols)
     wide = pl.ds(LEAD - 8, window(cols))
     pad = padded(cols)
@@ -272,7 +278,7 @@
     loads = [pltpu.make_async_copy(a, b, sem.at[i]) for i, (a, b) in enumerate(loads)]
     for copy in loads:
         copy.start()
-    for copy in loads:
+    for copy in loads[:14]:
         copy.wait()
     has_north = jnp.where(ids_ref[1] > 0, 1.0, 0.0)
     has_south = jnp.where(ids_ref[2] > 0, 1.0, 0.0)
@@ -287,6 +293,8 @@
 
     ends(advect, -3, 1)
     ends(advect_theta, -4, -3)
+    for copy in loads[14:]:
+        copy.wait()
     ends(wind_u, -2, 1)
     ends(wind_v, -3, 2)
     ends(theta, -2, 3)
@@ -294,21 +302,19 @@
     ends(wind_v, -1, 4)
     ends(theta, 0, 5)
 
-    @pl.when(ids_ref[3] != 0)
-    def _():
+    if near_pole:
         inside = pltpu.make_async_copy(
-            theta_ref.at[pl.ds(1, GROUP - 2)], send_ref.at[pl.ds(1, GROUP - 2), pl.ds(3 * pad, pad)], move_sem.at[0]
+            theta_ref.at[pl.ds(1, GROUP - 2)], out_ref.at[pl.ds(1, GROUP - 2), pl.ds(3 * pad, pad)], move_sem.at[0]
         )
         inside.start()
         for d in range(GROUP):
             for c, W in enumerate((A, B, C)):
-                send_ref[d, pl.ds(c * pad, cols)] = W[EDGE[d] + HALO, own]
+                out_ref[d, pl.ds(c * pad, cols)] = W[EDGE[d] + HALO, own]
         for d in (0, GROUP - 1):
-            send_ref[d, pl.ds(3 * pad, cols)] = C[INNER[d] + HALO, own]
+            out_ref[d, pl.ds(3 * pad, cols)] = C[INNER[d] + HALO, own]
         inside.wait()
-
-    @pl.when(ids_ref[3] == 0)
-    def _():
+    else:
+        hold, moved, out_sem = more
         inside = [
             pltpu.make_async_copy(ref, moved.at[:, pl.ds(c * pad, pad)], move_sem.at[c])
             for c, ref in enumerate((u_ref, v_ref, theta_ref))
@@ -331,20 +337,21 @@
             out.wait()
 
 
-def edge_rows(ids, metric, raw, rim, hn, hs, inner, after, cols, rows):
+def edge_rows(near_pole, ids, metric, raw, rim, hn, hs, inner, after, cols, rows):
     lev = raw.shape[-1]
     pad = padded(cols)
     whole = (3, cols * rows, lev)
-    return pl.pallas_call(
-        functools.partial(edge_kernel, cols, rows),
+    scratch = [pltpu.VMEM((rows + 2 * HALO, LEAD + window(cols), lev), f32)] * 6
+    scratch += [pltpu.SemaphoreType.DMA((20,)), pltpu.SemaphoreType.DMA((3,))]
+    if not near_pole:
+        scratch += [pltpu.VMEM(whole, f32), pltpu.VMEM((GROUP, 3 * pad, lev), f32), pltpu.SemaphoreType.DMA((3,))]
+    return pl.pallas_call(
+        functools.partial(edge_kernel, cols, rows, near_pole),
         in_specs=[smem(), smem()] + [any_space()] * 8,
-        out_specs=[vmem(), any_space()],
-        out_shape=[jax.ShapeDtypeStruct((GROUP, 4 * pad, lev), f32), jax.ShapeDtypeStruct(whole, f32)],
-        scratch_shapes=[pltpu.VMEM((rows + 2 * HALO, LEAD + window(cols), lev), f32)] * 6
-        + [pltpu.VMEM(whole, f32), pltpu.VMEM((GROUP, 3 * pad, lev), f32)]
-        + [pltpu.SemaphoreType.DMA((n,)) for n in (20, 3, 3)],
-        compiler_params=params(60),
-        cost_estimate=cost(8),
+        out_specs=vmem() if near_pole else any_space(),
+        out_shape=jax.ShapeDtypeStruct((GROUP, 4 * pad, lev) if near_pole else whole, f32),
+        scratch_shapes=scratch,
+        compiler_params=params(57 if near_pole else 60),
     )(ids, metric, raw, rim, hn, hs, *inner, after)
 
 
@@ -464,9 +471,15 @@
             xh = x.astype(bf16)
             xl = (x - xh.astype(f32)).astype(bf16)
             mh = matrix(hi_ref, e)
-            left = jnp.concatenate([mh, mh, matrix(lo_ref, e)], axis=1)
-            right = jnp.concatenate([xh, xl, xh], axis=0)
-            dst[:, lanes] = jnp.dot(left, right, preferred_element_type=f32)
+            ml = matrix(lo_ref, e)
+            if len(members) == 1:
+                both = jnp.dot(mh, jnp.concatenate([xh, xl], axis=1), preferred_element_type=f32)
+                small = jnp.dot(ml, xh, preferred_element_type=f32)
+                dst[:, lanes] = both[:, :lev] + (both[:, lev:] + small)
+            else:
+                left = jnp.concatenate([mh, mh, ml], axis=1)
+                right = jnp.concatenate([xh, xl, xh], axis=0)
+                dst[:, lanes] = jnp.dot(left, right, preferred_element_type=f32)
     for b in range(quarter):
         at = slice(b * cols, (b + 1) * cols)
         for i, u in enumerate(units):
@@ -592,22 +605,27 @@
     latitude = (-90.0 + (near.astype(f32) + 0.5) * (180.0 / total_lat)) * (jnp.pi / 180.0)
     metric = 1.0 / jnp.maximum(jnp.cos(latitude), 1.0 / CAP)
 
+    planes, own_north, own_south = split_planes(flat, (last, first), cols, rows)
+    send_north, send_south = with_columns(west, east_, own_north, own_south, cols, rows)
     wanted = jnp.stack([edge_row(me), inner_row(me)])
     chosen = wanted[:, None] == jnp.arange(rows, dtype=jnp.int32)[None, :]
     picked = jnp.sum(jnp.where(chosen, cutoffs.astype(f32)[None, :], 0.0), axis=1)
+    picked = tied(picked, send_north)
     offsets = offset_values(picked, total_lon)
     token = jnp.zeros((8, lev), f32)
     packed = offsets[1].reshape(GROUP * PACK, lev)
     hi, lo = skewed(offsets, token)
-    planes, own_north, own_south = split_planes(flat, (last, first), cols, rows)
-    send_north, send_south = with_columns(west, east_, own_north, own_south, cols, rows)
     halo_north = lax.ppermute(send_south, "lat", up)
     halo_south = lax.ppermute(send_north, "lat", down)
 
     u, v, theta, rim, raw = inner_rows(metric, planes, west, east_, packed, send_north, cols, rows)
     moved_u = lax.ppermute(u, "lat", outward)
     moved_v = lax.ppermute(v, "lat", outward)
-    pieces, other = edge_rows(ids, metric, raw, rim, halo_north, halo_south, (u, v, theta), lo, cols, rows)
+    def edges(near_pole, after):
+        inner = (u, v, theta)
+        return edge_rows(near_pole, ids, metric, raw, rim, halo_north, halo_south, inner, after, cols, rows)
+
+    pieces = edges(True, lo)
 
     def elsewhere(x, first, after):
         hi, lo = unpacked(first, total_lon, after)
@@ -617,7 +635,7 @@
         return hollow(x)
 
     def near_pole(x, after):
-        return swapped(filtered(((0, (0, 1, 2)), (1, (3,))), hi, lo, x, after, cols))
+        return swapped(filtered(((0, (0, 1)), (0, (2,)), (1, (3,))), hi, lo, x, after, cols))
 
     def same(x, *_):
         return x
@@ -627,6 +645,7 @@
     moved_back_u = lax.ppermute(back_u, "lat", inward)
     back_v = lax.cond(polar, idle, elsewhere, moved_v, moved_u, tied(token, whole))
     moved_back_v = lax.ppermute(back_v, "lat", inward)
+    other = edges(False, tied(token, back_v))
     pieces = lax.cond(polar, near_pole, same, whole, tied(token, back_v))
     return joined(ids, pieces, moved_back_u, moved_back_v, other, cols, rows).reshape(3, cols, rows, lev)
 

time: 157 us -> 153 us (0.975)
  matrix products: 3.99 us -> 2.33 us
  Pallas kernels: 40.6 us -> 39 us
    dot_general x2, matrix products: 3.99 us -> 2.33 us  [offset_values(): jnp.dot(factor, jnp.asarray(table), precision=lax.Precision.HIGHEST, pref...]
    pallas_call x1 -> x2, Pallas kernels: 7.14 us -> 7.23 us  [edge_rows(): pl.pallas_call(functools.partial(edge_kernel, cols, rows, near_pole), in_...]
  transfers between devices with their start and end apart: 8 -> 8, of which waited for: 2 -> 2; matrix products, arithmetic and copies ran while one was open for 5% -> 3% of each run, Pallas kernels for 22% -> 21%
where the time goes in v2:
time: 153 us; the launch traced here: 152 us
  blocking collectives  77.1 us (50%)
  Pallas kernels  39 us (25%)
  starting transfers between devices  19.1 us (12%)
  waiting for transfers between devices  7.68 us (5%)
  local copies, waits for them, and re-layouts  4.65 us (3%)
  matrix products  2.33 us (2%)
    all_to_all x2, blocking collectives, swapped(): return lax.all_to_all(x, 'lon', split_axis=0, concat_axis=0, tiled=True)  77.1 us
    pallas_call x1, Pallas kernels, inner_rows(): pl.pallas_call(functools.partial(inner_kernel, cols, rows), in_specs=[sme...  9.49 us
    pallas_call x2, Pallas kernels, edge_rows(): pl.pallas_call(functools.partial(edge_kernel, cols, rows, near_pole), in_...  7.23 us
    pallas_call x1, Pallas kernels, filtered(): pl.pallas_call(functools.partial(filter_kernel, groups, cols), in_specs=[...  7.19 us
    pallas_call x1, Pallas kernels, joined(): pl.pallas_call(functools.partial(join_kernel, cols, rows), in_specs=[smem...  5.13 us
    pallas_call x1, Pallas kernels, split_planes(): pl.pallas_call(functools.partial(split_kernel, cols, rows), in_specs=[any...  5.12 us
    ppermute x1, waiting for transfers between devices, body(): halo_south = lax.ppermute(send_north, 'lat', down)  4.38 us
    ppermute x1, starting transfers between devices, body(): halo_south = lax.ppermute(send_north, 'lat', down)  4.11 us
  transfers between devices with their start and end apart: 8, of which 2 were waited for; matrix products, arithmetic and copies ran while one was open for 3% of the time, Pallas kernels for 21%

profile of v2, /device:TPU:24, one launch (start us, length us, event | category | flops | bytes accessed | tf_op | source)
XLA Modules:
  0.0 152.2 jit_solution(14797776768029481960)
XLA Ops:
  0.0 1.0 fusion.14
  1.0 1.6 %collective-permute-start = (f32[3,80,128]{2,1,0:T(8,128)S(1)}, f32[3,80,128]{2,1,0:T(8,128)S(1)}, u32[]{:S(2)}, u32[]{:S(2)}) collective-permute-start(f32[3,80,128]{2,1,0:T(8,128)S(1)} %bitcast.15), channel_id=1, source_target_pairs={{0,1},{1,2},{2,3},{3,4},{4,5},{5,6},{6,7},{7,0},{8,9},{9,10},{10,1... | collective-permute-start | bytes 368648 | tf_op jit(solution)/shard_map/ppermute | solution.py:599
  2.6 3.6 %collective-permute-start.1 = (f32[3,80,128]{2,1,0:T(8,128)S(1)}, f32[3,80,128]{2,1,0:T(8,128)S(1)}, u32[]{:S(2)}, u32[]{:S(2)}) collective-permute-start(f32[3,80,128]{2,1,0:T(8,128)S(1)} %bitcast.13), channel_id=1, source_target_pairs={{1,0},{2,1},{3,2},{4,3},{5,4},{6,5},{7,6},{0,7},{9,8},{10,9},{11,1... | collective-permute-start | bytes 368648 | tf_op jit(solution)/shard_map/ppermute | solution.py:600
  6.1 0.6 maximum_divide_fusion.metric_ref.refs_0_
  6.8 5.1 %shard_map.64 = (f32[3,16,200,128]{3,2,1,0:T(8,128)}, f32[13,200,128]{2,1,0:T(8,128)}, f32[13,200,128]{2,1,0:T(8,128)}) custom-call(f32[3,2880,128]{2,1,0:T(8,128)} %bitcast.12, f32[3,80,128]{2,1,0:T(8,128)} %bitcast.16, f32[3,80,128]{2,1,0:T(8,128)} %bitcast.14), custom_call_target="tpu_custom_call" | custom-call | tf_op jit(solution)/shard_map/pallas_call | solution.py:96
  12.2 2.0 %shard_map.65 = (f32[13,200,128]{2,1,0:T(8,128)}, f32[13,200,128]{2,1,0:T(8,128)}) custom-call(f32[3,80,128]{2,1,0:T(8,128)S(1)} %collective-permute-done.west_ref, f32[3,80,128]{2,1,0:T(8,128)S(1)} %collective-permute-done.1.east_ref, f32[13,200,128]{2,1,0:T(8,128)} %get-tuple-element.64._, ...), custom_call_target="tpu_custom_call", output_to_operand_aliasing={{0}: (2, {}), {1}: (3, {})} | custom-call | tf_op jit(solution)/shard_map/pallas_call | solution.py:135
  14.2 4.1 %collective-permute-start.3 = (f32[13,200,128]{2,1,0:T(8,128)}, f32[13,200,128]{2,1,0:T(8,128)S(1)}, u32[]{:S(2)}, u32[]{:S(2)}) collective-permute-start(f32[13,200,128]{2,1,0:T(8,128)} %get-tuple-element.66._), channel_id=1, source_target_pairs={{8,0},{16,8},{24,16},{32,24},{40,32},{48,40},{56,48},{64,56},{72,6... | collective-permute-start | bytes 3993608 | tf_op jit(solution)/shard_map/ppermute | solution.py:619
  18.3 1.9 %collective-permute-start.2 = (f32[13,200,128]{2,1,0:T(8,128)}, f32[13,200,128]{2,1,0:T(8,128)S(1)}, u32[]{:S(2)}, u32[]{:S(2)}) collective-permute-start(f32[13,200,128]{2,1,0:T(8,128)} %get-tuple-element.69), channel_id=1, source_target_pairs={{0,8},{8,16},{16,24},{24,32},{32,40},{40,48},{48,56},{56,64},{64,7... | collective-permute-start | bytes 3993608 | tf_op jit(solution)/shard_map/ppermute | solution.py:618
  20.3 1.2 fusion.2
  21.5 1.2 fusion.1
  22.7 0.6 reshape_squeeze.3.off_ref
  23.3 9.5 %shard_map.67 = (f32[8,184,128]{2,1,0:T(8,128)}, f32[8,184,128]{2,1,0:T(8,128)}, f32[8,184,128]{2,1,0:T(8,128)}, f32[3,10,200,128]{3,2,1,0:T(8,128)}, f32[3,4,200,128]{3,2,1,0:T(8,128)}) custom-call(f32[26]{0:T(128)} %maximum_divide_fusion.metric_ref.refs_0_, f32[3,16,200,128]{3,2,1,0:T(8,128)} %get-tuple-element.63.planes_ref, f32[3,80,128]{2,1,0:T(8,128)} %copy-done, ...), custom_call_target="tpu_custom_call" | custom-call | bytes 33210000 | tf_op jit(solution)/shard_map/pallas_call | solution.py:241
  32.8 3.2 %collective-permute-start.4 = (f32[8,184,128]{2,1,0:T(8,128)}, f32[8,184,128]{2,1,0:T(8,128)}, u32[]{:S(2)}, u32[]{:S(2)}) collective-permute-start(f32[8,184,128]{2,1,0:T(8,128)} %get-tuple-element.70.refs_5_), channel_id=1, source_target_pairs={{0,32},{8,40},{16,48},{24,56},{96,64},{104,72},{112,80},{120,88},{... | collective-permute-start | bytes 2261000 | tf_op jit(solution)/shard_map/ppermute | solution.py:622
  36.1 2.2 %collective-permute-start.5 = (f32[8,184,128]{2,1,0:T(8,128)}, f32[8,184,128]{2,1,0:T(8,128)}, u32[]{:S(2)}, u32[]{:S(2)}) collective-permute-start(f32[8,184,128]{2,1,0:T(8,128)} %get-tuple-element.71.refs_6_), channel_id=1, source_target_pairs={{0,32},{8,40},{16,48},{24,56},{96,64},{104,72},{112,80},{120,88},{... | collective-permute-start | bytes 2261000 | tf_op jit(solution)/shard_map/ppermute | solution.py:623
  38.3 0.6 pad_add_fusion.ids_ref
  38.9 2.8 %shard_map.68 = (bf16[2,2,128,1408]{3,2,1,0:T(8,128)(2,1)}, bf16[2,2,128,1408]{3,2,1,0:T(8,128)(2,1)S(1)}) custom-call(f32[2,2,1,1536]{3,2,1,0:T(1,128)S(1)} %broadcast_in_dim.39.p_ref, f32[8,128]{1,0:T(8,128)S(1)} %broadcast_in_dim.40._.x_ref), custom_call_target="tpu_custom_call" | custom-call | tf_op jit(solution)/shard_map/pallas_call | solution.py:434
  41.8 4.4 %collective-permute-done.3.refs_4_ = f32[13,200,128]{2,1,0:T(8,128)S(1)} collective-permute-done((f32[13,200,128]{2,1,0:T(8,128)}, f32[13,200,128]{2,1,0:T(8,128)S(1)}, u32[]{:S(2)}, u32[]{:S(2)}) %collective-permute-start.3) | collective-permute-done | bytes 1331232 | tf_op jit(solution)/shard_map/ppermute | solution.py:619
  46.1 3.3 %collective-permute-done.2.refs_3_ = f32[13,200,128]{2,1,0:T(8,128)S(1)} collective-permute-done((f32[13,200,128]{2,1,0:T(8,128)}, f32[13,200,128]{2,1,0:T(8,128)S(1)}, u32[]{:S(2)}, u32[]{:S(2)}) %collective-permute-start.2) | collective-permute-done | bytes 1331232 | tf_op jit(solution)/shard_map/ppermute | solution.py:618
  49.4 1.1 copy-done.6
  50.5 6.2 %shard_map.69 = f32[8,736,128]{2,1,0:T(8,128)S(1)} custom-call(s32[4]{0:T(128)} %pad_add_fusion.ids_ref, f32[26]{0:T(128)} %maximum_divide_fusion.metric_ref.refs_0_, f32[3,4,200,128]{3,2,1,0:T(8,128)} %get-tuple-element.67.refs_1_, f32[3,10,200,128]{3,2,1,0:T(8,128)} %get-tuple-element.68.refs_2_, f32[13,200,128]{2,1,0:T(8,128)} %copy-done.6, ...), custom_call_target="tpu_custom_call" | custom-call | tf_op jit(solution)/shard_map/pallas_call | solution.py:348
  56.7 39.5 %conditional.4 = (f32[8,736,128]{2,1,0:T(8,128)S(1)}) conditional(s32[]{:T(128)} %convert_element_type.6, f32[8,736,128]{2,1,0:T(8,128)S(1)} %shard_map.69, f32[8,736,128]{2,1,0:T(8,128)S(1)} %shard_map.69), branch_computations={%region_1.2_spmd, %region_2.3_spmd} | conditional | bytes 12058632 | solution.py:643
  56.7 0.2 copy.27
  56.9 39.2 %all_to_all.24 = f32[8,736,128]{2,1,0:T(8,128)S(1)} all-to-all(f32[8,736,128]{2,1,0:T(8,128)S(1)} %copy.27), channel_id=1, replica_groups=mesh['lat'=16,'lon'=8] {'lon'}, dimensions={0} | all-to-all | bytes 6029312 | tf_op jit(solution)/shard_map/cond/branch_1_fun/all_to_all | solution.py:576
  96.2 1.7 %copy-done.3 = f32[8,736,128]{2,1,0:T(8,128)} copy-done((f32[8,736,128]{2,1,0:T(8,128)}, f32[8,736,128]{2,1,0:T(8,128)S(1)}, u32[]{:S(2)}) %copy-start.3) | copy-done | bytes 3014680
  97.9 1.3 collective-permute-start.6
  99.2 0.2 conditional.5
  99.4 1.3 collective-permute-start.7
  100.7 45.1 %conditional.6 = (f32[8,736,128]{2,1,0:T(8,128)}) conditional(s32[]{:T(128)} %convert_element_type.6, f32[8,736,128]{2,1,0:T(8,128)} %copy-done.3, (bf16[2,2,128,1408]{3,2,1,0:T(8,128)(2,1)}, bf16[2,2,128,1408]{3,2,1,0:T(8,128)(2,1)}, f32[8,736,128]{2,1,0:T(8,128)}, f32[8,128]{1,0:T(8,128)S(1)}) %tuple.44), branch_computations={%region_5.6_spmd, %region_6.7_spmd} | conditional | bytes 6029320 | solution.py:649
  100.7 7.2 %branch_1_fun.4 = f32[8,736,128]{2,1,0:T(8,128)S(1)} custom-call(bf16[2,2,128,1408]{3,2,1,0:T(8,128)(2,1)} %get-tuple-element.43.hi_ref, bf16[2,2,128,1408]{3,2,1,0:T(8,128)(2,1)} %get-tuple-element.44.lo_ref, f32[8,736,128]{2,1,0:T(8,128)} %get-tuple-element.45.x_ref, f32[8,128]{1,0:T(8,128)S(1)} %get-tuple-element.46._), custom_call_target="tpu_custom_call" | custom-call | tf_op jit(solution)/shard_map/cond/branch_1_fun/pallas_call | solution.py:497
  107.9 37.9 %all_to_all.26 = f32[8,736,128]{2,1,0:T(8,128)} all-to-all(f32[8,736,128]{2,1,0:T(8,128)S(1)} %branch_1_fun.4), channel_id=1, replica_groups=mesh['lat'=16,'lon'=8] {'lon'}, dimensions={0} | all-to-all | bytes 6029312 | tf_op jit(solution)/shard_map/cond/branch_1_fun/all_to_all | solution.py:576
  145.8 1.0 shard_map.72._
  146.9 5.1 %shard_map.73 = f32[3,2880,128]{2,1,0:T(8,128)} custom-call(s32[4]{0:T(128)S(1)} %copy-done.2, f32[8,736,128]{2,1,0:T(8,128)} %get-tuple-element.79.y_ref, f32[8,184,128]{2,1,0:T(8,128)S(1)} %collective-permute-done.6.u_ref, f32[8,184,128]{2,1,0:T(8,128)S(1)} %collective-permute-done.7.v_ref, ...), custom_call_target="tpu_custom_call", output_to_operand_aliasing={{}: (4, {})} | custom-call | tf_op jit(solution)/shard_map/pallas_call | solution.py:530
  (52 shorter events, 0.5 us)
Async XLA Ops:
  1.0 5.8 %copy-start.9 = (f32[3,5,16,128]{3,2,1,0:T(8,128)}, f32[3,5,16,128]{3,2,1,0:T(8,128)S(1)}, u32[]{:S(2)}) copy-start(f32[3,5,16,128]{3,2,1,0:T(8,128)S(1)} %get-tuple-element.75) | copy-start | bytes 368644
  1.0 5.8 %copy-start.10 = (f32[3,5,16,128]{3,2,1,0:T(8,128)}, f32[3,5,16,128]{3,2,1,0:T(8,128)S(1)}, u32[]{:S(2)}) copy-start(f32[3,5,16,128]{3,2,1,0:T(8,128)S(1)} %get-tuple-element.76) | copy-start | bytes 368644
  1.0 11.1 %collective-permute-start = (f32[3,80,128]{2,1,0:T(8,128)S(1)}, f32[3,80,128]{2,1,0:T(8,128)S(1)}, u32[]{:S(2)}, u32[]{:S(2)}) collective-permute-start(f32[3,80,128]{2,1,0:T(8,128)S(1)} %bitcast.15), channel_id=1, source_target_pairs={{0,1},{1,2},{2,3},{3,4},{4,5},{5,6},{6,7},{7,0},{8,9},{9,10},{10,1... | collective-permute-start | bytes 368648 | tf_op jit(solution)/shard_map/ppermute | solution.py:599
  2.6 9.6 %collective-permute-start.1 = (f32[3,80,128]{2,1,0:T(8,128)S(1)}, f32[3,80,128]{2,1,0:T(8,128)S(1)}, u32[]{:S(2)}, u32[]{:S(2)}) collective-permute-start(f32[3,80,128]{2,1,0:T(8,128)S(1)} %bitcast.13), channel_id=1, source_target_pairs={{1,0},{2,1},{3,2},{4,3},{5,4},{6,5},{7,6},{0,7},{9,8},{10,9},{11,1... | collective-permute-start | bytes 368648 | tf_op jit(solution)/shard_map/ppermute | solution.py:600
  6.8 5.1 %copy-start.15 = (s32[16]{0:T(128)S(1)}, s32[16]{0:T(128)}, u32[]{:S(2)}) copy-start(s32[16]{0:T(128)} %param.15) | copy-start | bytes 196
  11.9 8.3 %copy-start.7 = (f32[361,1536]{1,0:T(8,128)S(1)}, f32[361,1536]{1,0:T(8,128)}, u32[]{:S(2)}) copy-start(f32[361,1536]{1,0:T(8,128)} %constant.47.clone) | copy-start | bytes 6653956
  11.9 8.3 %copy-start.13 = (f32[361]{0:T(512)S(1)}, f32[361]{0:T(512)}, u32[]{:S(2)}) copy-start(f32[361]{0:T(512)} %constant.46.clone) | copy-start | bytes 4336
  11.9 8.3 %copy-start.14 = (f32[361]{0:T(512)S(1)}, f32[361]{0:T(512)}, u32[]{:S(2)}) copy-start(f32[361]{0:T(512)} %constant.53) | copy-start | bytes 4336
  12.2 9.3 %copy-start = (f32[3,80,128]{2,1,0:T(8,128)}, f32[3,80,128]{2,1,0:T(8,128)S(1)}, u32[]{:S(2)}) copy-start(f32[3,80,128]{2,1,0:T(8,128)S(1)} %collective-permute-done.west_ref) | copy-start | bytes 368644
  12.2 9.3 %copy-start.1 = (f32[3,80,128]{2,1,0:T(8,128)}, f32[3,80,128]{2,1,0:T(8,128)S(1)}, u32[]{:S(2)}) copy-start(f32[3,80,128]{2,1,0:T(8,128)S(1)} %collective-permute-done.1.east_ref) | copy-start | bytes 368644
  14.2 7.3 %copy-start.8 = (f32[360,1536]{1,0:T(8,128)S(1)}, f32[360,1536]{1,0:T(8,128)}, u32[]{:S(2)}) copy-start(f32[360,1536]{1,0:T(8,128)} %constant.49.clone) | copy-start | bytes 6635524
  14.2 7.3 %copy-start.11 = (f32[360]{0:T(512)S(1)}, f32[360]{0:T(512)}, u32[]{:S(2)}) copy-start(f32[360]{0:T(512)} %constant.48.clone) | copy-start | bytes 4324
  14.2 7.3 %copy-start.12 = (f32[360]{0:T(512)S(1)}, f32[360]{0:T(512)}, u32[]{:S(2)}) copy-start(f32[360]{0:T(512)} %constant.54) | copy-start | bytes 4324
  14.2 31.9 %collective-permute-start.3 = (f32[13,200,128]{2,1,0:T(8,128)}, f32[13,200,128]{2,1,0:T(8,128)S(1)}, u32[]{:S(2)}, u32[]{:S(2)}) collective-permute-start(f32[13,200,128]{2,1,0:T(8,128)} %get-tuple-element.66._), channel_id=1, source_target_pairs={{8,0},{16,8},{24,16},{32,24},{40,32},{48,40},{56,48},{64,56},{72,6... | collective-permute-start | bytes 3993608 | tf_op jit(solution)/shard_map/ppermute | solution.py:619
  18.3 31.1 %collective-permute-start.2 = (f32[13,200,128]{2,1,0:T(8,128)}, f32[13,200,128]{2,1,0:T(8,128)S(1)}, u32[]{:S(2)}, u32[]{:S(2)}) collective-permute-start(f32[13,200,128]{2,1,0:T(8,128)} %get-tuple-element.69), channel_id=1, source_target_pairs={{0,8},{8,16},{16,24},{24,32},{32,40},{40,48},{48,56},{56,64},{64,7... | collective-permute-start | bytes 3993608 | tf_op jit(solution)/shard_map/ppermute | solution.py:618
  32.8 63.4 %collective-permute-start.4 = (f32[8,184,128]{2,1,0:T(8,128)}, f32[8,184,128]{2,1,0:T(8,128)}, u32[]{:S(2)}, u32[]{:S(2)}) collective-permute-start(f32[8,184,128]{2,1,0:T(8,128)} %get-tuple-element.70.refs_5_), channel_id=1, source_target_pairs={{0,32},{8,40},{16,48},{24,56},{96,64},{104,72},{112,80},{120,88},{... | collective-permute-start | bytes 2261000 | tf_op jit(solution)/shard_map/ppermute | solution.py:622
  36.1 63.1 %collective-permute-start.5 = (f32[8,184,128]{2,1,0:T(8,128)}, f32[8,184,128]{2,1,0:T(8,128)}, u32[]{:S(2)}, u32[]{:S(2)}) collective-permute-start(f32[8,184,128]{2,1,0:T(8,128)} %get-tuple-element.71.refs_6_), channel_id=1, source_target_pairs={{0,32},{8,40},{16,48},{24,56},{96,64},{104,72},{112,80},{120,88},{... | collective-permute-start | bytes 2261000 | tf_op jit(solution)/shard_map/ppermute | solution.py:623
  41.8 15.0 %copy-start.4 = (bf16[2,2,128,1408]{3,2,1,0:T(8,128)(2,1)}, bf16[2,2,128,1408]{3,2,1,0:T(8,128)(2,1)S(1)}, u32[]{:S(2)}) copy-start(bf16[2,2,128,1408]{3,2,1,0:T(8,128)(2,1)S(1)} %get-tuple-element.73.refs_8_) | copy-start | bytes 4325380
  46.1 3.3 %copy-start.5 = (f32[13,200,128]{2,1,0:T(8,128)}, f32[13,200,128]{2,1,0:T(8,128)S(1)}, u32[]{:S(2)}) copy-start(f32[13,200,128]{2,1,0:T(8,128)S(1)} %collective-permute-done.3.refs_4_) | copy-start | bytes 3993604
  49.4 1.1 copy-start.6
  96.2 1.7 %copy-start.3 = (f32[8,736,128]{2,1,0:T(8,128)}, f32[8,736,128]{2,1,0:T(8,128)S(1)}, u32[]{:S(2)}) copy-start(f32[8,736,128]{2,1,0:T(8,128)S(1)} %get-tuple-element.77._) | copy-start | bytes 9043972
  97.9 49.0 %collective-permute-start.6 = (f32[8,184,128]{2,1,0:T(8,128)}, f32[8,184,128]{2,1,0:T(8,128)S(1)}, u32[]{:S(2)}, u32[]{:S(2)}) collective-permute-start(f32[8,184,128]{2,1,0:T(8,128)} %get-tuple-element.80), channel_id=1, source_target_pairs={{32,0},{40,8},{48,16},{56,24},{64,96},{72,104},{80,112},{88,120},{... | collective-permute-start | bytes 2261000 | tf_op jit(solution)/shard_map/ppermute | solution.py:645
  99.4 47.5 %collective-permute-start.7 = (f32[8,184,128]{2,1,0:T(8,128)S(1)}, f32[8,184,128]{2,1,0:T(8,128)S(1)}, u32[]{:S(2)}, u32[]{:S(2)}) collective-permute-start(f32[8,184,128]{2,1,0:T(8,128)S(1)} %get-tuple-element.78._), channel_id=1, source_target_pairs={{32,0},{40,8},{48,16},{56,24},{64,96},{72,104},{80,112},{88,120},{... | collective-permute-start | bytes 2261000 | tf_op jit(solution)/shard_map/ppermute | solution.py:647
  145.8 1.1 copy-start.2

commit v3 on v2

--- a/solution.py
+++ b/solution.py
@@ -15,7 +15,7 @@
 CAP = 2.0
 LEAD = 16
 GROUP = 8
-UNROLL = 2
+UNROLL = 4
 PACK = 3
 MIB = 1024 * 1024
 
@@ -625,8 +625,6 @@
         inner = (u, v, theta)
         return edge_rows(near_pole, ids, metric, raw, rim, halo_north, halo_south, inner, after, cols, rows)
 
-    pieces = edges(True, lo)
-
     def elsewhere(x, first, after):
         hi, lo = unpacked(first, total_lon, after)
         return swapped(filtered(((0, (0,)),), hi, lo, swapped(x), after, cols))
@@ -640,12 +638,16 @@
     def same(x, *_):
         return x
 
-    whole = lax.cond(polar, swapped, same, pieces)
+    def first_half(after):
+        return swapped(edges(True, after))
+
+    blank = jax.ShapeDtypeStruct((GROUP, 4 * padded(cols), lev), f32)
+    whole = lax.cond(polar, first_half, lambda _: hollow(blank), lo)
     back_u = lax.cond(polar, idle, elsewhere, moved_u, moved_u, tied(token, whole))
     moved_back_u = lax.ppermute(back_u, "lat", inward)
     back_v = lax.cond(polar, idle, elsewhere, moved_v, moved_u, tied(token, whole))
     moved_back_v = lax.ppermute(back_v, "lat", inward)
-    other = edges(False, tied(token, back_v))
+    other = lax.cond(polar, lambda _: hollow(flat), lambda after: edges(False, after), tied(token, back_v))
     pieces = lax.cond(polar, near_pole, same, whole, tied(token, back_v))
     return joined(ids, pieces, moved_back_u, moved_back_v, other, cols, rows).reshape(3, cols, rows, lev)
 

time: 153 us -> 151 us (0.987)
  local copies, waits for them, and re-layouts: 4.65 us -> 1.69 us
  blocking collectives: 77.1 us -> 78.9 us
    ppermute x1, waiting for transfers between devices: 3.29 us -> 8.53 us  [body(): halo_north = lax.ppermute(send_south, 'lat', up)]
    ppermute x1, waiting for transfers between devices: 4.38 us -> 0.01 us  [body(): halo_south = lax.ppermute(send_north, 'lat', down)]
    unnamed x32 -> x20, local copies, waits for them, and re-layouts: 2.82 us -> 0.06 us
    all_to_all x2, blocking collectives: 77.1 us -> 78.9 us  [swapped(): return lax.all_to_all(x, 'lon', split_axis=0, concat_axis=0, tiled=True)]
    pallas_call x2 -> x1, Pallas kernels: 7.23 us -> 7.08 us  [edge_rows(): pl.pallas_call(functools.partial(edge_kernel, cols, rows, near_pole), in_...]
  transfers between devices with their start and end apart: 8 -> 8, of which waited for: 2 -> 1; matrix products, arithmetic and copies ran while one was open for 3% -> 3% of each run, Pallas kernels for 21% -> 21%
where the time goes in v3:
time: 151 us
  blocking collectives  78.9 us (52%)
  Pallas kernels  39.4 us (26%)
  starting transfers between devices  18.3 us (12%)
  waiting for transfers between devices  8.55 us (6%)
  matrix products  2.33 us (2%)
  local copies, waits for them, and re-layouts  1.69 us (1%)
    all_to_all x2, blocking collectives, swapped(): return lax.all_to_all(x, 'lon', split_axis=0, concat_axis=0, tiled=True)  78.9 us
    pallas_call x1, Pallas kernels, inner_rows(): pl.pallas_call(functools.partial(inner_kernel, cols, rows), in_specs=[sme...  9.67 us
    ppermute x1, waiting for transfers between devices, body(): halo_north = lax.ppermute(send_south, 'lat', up)  8.53 us
    pallas_call x1, Pallas kernels, filtered(): pl.pallas_call(functools.partial(filter_kernel, groups, cols), in_specs=[...  7.19 us
    pallas_call x1, Pallas kernels, edge_rows(): pl.pallas_call(functools.partial(edge_kernel, cols, rows, near_pole), in_...  7.08 us
    pallas_call x1, Pallas kernels, joined(): pl.pallas_call(functools.partial(join_kernel, cols, rows), in_specs=[smem...  5.13 us
    pallas_call x1, Pallas kernels, split_planes(): pl.pallas_call(functools.partial(split_kernel, cols, rows), in_specs=[any...  5.13 us
    ppermute x1, starting transfers between devices, body(): halo_south = lax.ppermute(send_north, 'lat', down)  4.11 us
  transfers between devices with their start and end apart: 8, of which 1 were waited for; matrix products, arithmetic and copies ran while one was open for 3% of the time, Pallas kernels for 21%

profile of v3, /device:TPU:24, one launch (start us, length us, event | category | flops | bytes accessed | tf_op | source)
XLA Modules:
  0.0 150.8 jit_solution(9547253578011436351)
XLA Ops:
  0.0 1.0 fusion.14
  1.0 1.6 %collective-permute-start = (f32[3,80,128]{2,1,0:T(8,128)S(1)}, f32[3,80,128]{2,1,0:T(8,128)S(1)}, u32[]{:S(2)}, u32[]{:S(2)}) collective-permute-start(f32[3,80,128]{2,1,0:T(8,128)S(1)} %bitcast.15), channel_id=1, source_target_pairs={{0,1},{1,2},{2,3},{3,4},{4,5},{5,6},{6,7},{7,0},{8,9},{9,10},{10,1... | collective-permute-start | bytes 368648 | tf_op jit(solution)/shard_map/ppermute | solution.py:599
  2.6 3.6 %collective-permute-start.1 = (f32[3,80,128]{2,1,0:T(8,128)S(1)}, f32[3,80,128]{2,1,0:T(8,128)S(1)}, u32[]{:S(2)}, u32[]{:S(2)}) collective-permute-start(f32[3,80,128]{2,1,0:T(8,128)S(1)} %bitcast.13), channel_id=1, source_target_pairs={{1,0},{2,1},{3,2},{4,3},{5,4},{6,5},{7,6},{0,7},{9,8},{10,9},{11,1... | collective-permute-start | bytes 368648 | tf_op jit(solution)/shard_map/ppermute | solution.py:600
  6.2 0.1 pad_add_fusion.1
  6.2 0.7 convert_element_type.16
  6.9 5.1 %shard_map.64 = (f32[3,16,200,128]{3,2,1,0:T(8,128)}, f32[13,200,128]{2,1,0:T(8,128)}, f32[13,200,128]{2,1,0:T(8,128)}) custom-call(f32[3,2880,128]{2,1,0:T(8,128)} %bitcast.12, f32[3,80,128]{2,1,0:T(8,128)} %bitcast.16, f32[3,80,128]{2,1,0:T(8,128)} %bitcast.14), custom_call_target="tpu_custom_call" | custom-call | tf_op jit(solution)/shard_map/pallas_call | solution.py:96
  12.0 0.0 copy-start.4
  12.1 0.0 copy-start.9
  12.1 0.0 copy-start.10
  12.1 0.2 fusion.11.x_ref
  12.3 1.9 %shard_map.65 = (f32[13,200,128]{2,1,0:T(8,128)}, f32[13,200,128]{2,1,0:T(8,128)}) custom-call(f32[3,80,128]{2,1,0:T(8,128)S(1)} %collective-permute-done.west_ref, f32[3,80,128]{2,1,0:T(8,128)S(1)} %collective-permute-done.1.east_ref, f32[13,200,128]{2,1,0:T(8,128)} %get-tuple-element.125._, ...), custom_call_target="tpu_custom_call", output_to_operand_aliasing={{0}: (2, {}), {1}: (3, {})} | custom-call | tf_op jit(solution)/shard_map/pallas_call | solution.py:135
  14.2 0.0 copy-start.3
  14.3 4.1 %collective-permute-start.3 = (f32[13,200,128]{2,1,0:T(8,128)}, f32[13,200,128]{2,1,0:T(8,128)}, u32[]{:S(2)}, u32[]{:S(2)}) collective-permute-start(f32[13,200,128]{2,1,0:T(8,128)} %get-tuple-element.127._), channel_id=1, source_target_pairs={{8,0},{16,8},{24,16},{32,24},{40,32},{48,40},{56,48},{64,56},{72,6... | collective-permute-start | bytes 3993608 | tf_op jit(solution)/shard_map/ppermute | solution.py:619
  18.4 1.9 %collective-permute-start.2 = (f32[13,200,128]{2,1,0:T(8,128)}, f32[13,200,128]{2,1,0:T(8,128)}, u32[]{:S(2)}, u32[]{:S(2)}) collective-permute-start(f32[13,200,128]{2,1,0:T(8,128)} %get-tuple-element.130), channel_id=1, source_target_pairs={{0,8},{8,16},{16,24},{24,32},{32,40},{40,48},{48,56},{56,64},{64,7... | collective-permute-start | bytes 3993608 | tf_op jit(solution)/shard_map/ppermute | solution.py:618
  20.4 1.2 fusion.1
  21.6 1.2 fusion.2
  22.8 0.6 reshape_squeeze.3.off_ref
  23.4 9.7 %shard_map.67 = (f32[8,184,128]{2,1,0:T(8,128)}, f32[8,184,128]{2,1,0:T(8,128)}, f32[8,184,128]{2,1,0:T(8,128)}, f32[3,10,200,128]{3,2,1,0:T(8,128)}, f32[3,4,200,128]{3,2,1,0:T(8,128)}) custom-call(f32[26]{0:T(128)S(1)} %maximum_divide_fusion.metric_ref, f32[3,16,200,128]{3,2,1,0:T(8,128)} %get-tuple-element.124.planes_ref, f32[3,80,128]{2,1,0:T(8,128)} %copy-done, ...), custom_call_target="tpu_custom_call" | custom-call | bytes 33210000 | tf_op jit(solution)/shard_map/pallas_call | solution.py:241
  33.1 2.4 %collective-permute-start.4 = (f32[8,184,128]{2,1,0:T(8,128)}, f32[8,184,128]{2,1,0:T(8,128)S(1)}, u32[]{:S(2)}, u32[]{:S(2)}) collective-permute-start(f32[8,184,128]{2,1,0:T(8,128)} %get-tuple-element.131), channel_id=1, source_target_pairs={{0,32},{8,40},{16,48},{24,56},{96,64},{104,72},{112,80},{120,88},{... | collective-permute-start | bytes 2261000 | tf_op jit(solution)/shard_map/ppermute | solution.py:622
  35.5 2.2 %collective-permute-start.5 = (f32[8,184,128]{2,1,0:T(8,128)}, f32[8,184,128]{2,1,0:T(8,128)}, u32[]{:S(2)}, u32[]{:S(2)}) collective-permute-start(f32[8,184,128]{2,1,0:T(8,128)} %get-tuple-element.132), channel_id=1, source_target_pairs={{0,32},{8,40},{16,48},{24,56},{96,64},{104,72},{112,80},{120,88},{... | collective-permute-start | bytes 2261000 | tf_op jit(solution)/shard_map/ppermute | solution.py:623
  37.7 0.1 pad_add_fusion.ids_ref
  37.8 3.3 %shard_map.68 = (bf16[2,2,128,1408]{3,2,1,0:T(8,128)(2,1)}, bf16[2,2,128,1408]{3,2,1,0:T(8,128)(2,1)}) custom-call(f32[2,2,1,1536]{3,2,1,0:T(1,128)S(1)} %broadcast_in_dim.39.p_ref, f32[8,128]{1,0:T(8,128)S(1)} %broadcast_in_dim.40._.x_ref), custom_call_target="tpu_custom_call" | custom-call | tf_op jit(solution)/shard_map/pallas_call | solution.py:434
  41.1 8.5 %collective-permute-done.2 = f32[13,200,128]{2,1,0:T(8,128)} collective-permute-done((f32[13,200,128]{2,1,0:T(8,128)}, f32[13,200,128]{2,1,0:T(8,128)}, u32[]{:S(2)}, u32[]{:S(2)}) %collective-permute-start.2) | collective-permute-done | bytes 1331232 | tf_op jit(solution)/shard_map/ppermute | solution.py:618
  49.6 47.7 %conditional.5 = (f32[8,736,128]{2,1,0:T(8,128)}) conditional(s32[]{:T(128)} %convert_element_type.6, () %tuple.35, (s32[4]{0:T(128)S(1)}, f32[26]{0:T(128)S(1)}, f32[3,4,200,128]{3,2,1,0:T(8,128)}, f32[3,10,200,128]{3,2,1,0:T(8,128)}, f32[13,200,128]{2,1,0:T(8,128)}, /*index=5*/f32[13,200,128]{2,1,0:T(8,128)}, f32[8,184,128]{2,1,0:T(8,128)}, ...), branch_computations={%region_1.2_spmd, %region_2.3_spmd} | conditional | bytes 6029320 | solution.py:645
  49.6 7.1 %branch_1_fun.5 = f32[8,736,128]{2,1,0:T(8,128)} custom-call(s32[4]{0:T(128)S(1)} %get-tuple-element.76.ids_ref, f32[26]{0:T(128)S(1)} %get-tuple-element.78.refs_0_, f32[3,4,200,128]{3,2,1,0:T(8,128)} %get-tuple-element.80.refs_1_, f32[3,10,200,128]{3,2,1,0:T(8,128)} %get-tuple-element.82.refs_2_, f32[13,200,128]{2,1,0:T(8,128)} %get-tuple-element.83.refs_3_, ...), custom_call_target="tpu_custom_call" | custom-call | tf_op jit(solution)/shard_map/cond/branch_1_fun/pallas_call | solution.py:348
  56.7 40.6 %all_to_all.24 = f32[8,736,128]{2,1,0:T(8,128)} all-to-all(f32[8,736,128]{2,1,0:T(8,128)} %branch_1_fun.5), channel_id=1, replica_groups=mesh['lat'=16,'lon'=8] {'lon'}, dimensions={0} | all-to-all | bytes 6029312 | tf_op jit(solution)/shard_map/cond/branch_1_fun/all_to_all | solution.py:576
  97.3 1.3 collective-permute-start.6
  98.7 1.3 collective-permute-start.7
  100.0 45.5 %conditional.7 = (f32[8,736,128]{2,1,0:T(8,128)}) conditional(s32[]{:T(128)} %convert_element_type.6, f32[8,736,128]{2,1,0:T(8,128)} %get-tuple-element.138._, (bf16[2,2,128,1408]{3,2,1,0:T(8,128)(2,1)}, bf16[2,2,128,1408]{3,2,1,0:T(8,128)(2,1)}, f32[8,736,128]{2,1,0:T(8,128)}, f32[8,128]{1,0:T(8,128)S(1)}) %tuple.39), branch_computations={%region_5.6_spmd, %region_6.7_spmd} | conditional | bytes 6029320 | solution.py:651
  100.0 7.2 %branch_1_fun.7 = f32[8,736,128]{2,1,0:T(8,128)S(1)} custom-call(bf16[2,2,128,1408]{3,2,1,0:T(8,128)(2,1)} %get-tuple-element.94.hi_ref, bf16[2,2,128,1408]{3,2,1,0:T(8,128)(2,1)} %get-tuple-element.95.lo_ref, f32[8,736,128]{2,1,0:T(8,128)} %get-tuple-element.96.x_ref, f32[8,128]{1,0:T(8,128)S(1)} %get-tuple-element.97._), custom_call_target="tpu_custom_call" | custom-call | tf_op jit(solution)/shard_map/cond/branch_1_fun/pallas_call | solution.py:497
  107.2 38.3 %all_to_all.26 = f32[8,736,128]{2,1,0:T(8,128)} all-to-all(f32[8,736,128]{2,1,0:T(8,128)S(1)} %branch_1_fun.7), channel_id=1, replica_groups=mesh['lat'=16,'lon'=8] {'lon'}, dimensions={0} | all-to-all | bytes 6029312 | tf_op jit(solution)/shard_map/cond/branch_1_fun/all_to_all | solution.py:576
  145.5 5.1 %shard_map.71 = f32[3,2880,128]{2,1,0:T(8,128)} custom-call(s32[4]{0:T(128)S(1)} %pad_add_fusion.ids_ref, f32[8,736,128]{2,1,0:T(8,128)} %get-tuple-element.140.y_ref, f32[8,184,128]{2,1,0:T(8,128)S(1)} %collective-permute-done.6.u_ref, f32[8,184,128]{2,1,0:T(8,128)S(1)} %collective-permute-done.7.v_ref, ...), custom_call_target="tpu_custom_call", output_to_operand_aliasing={{}: (4, {})} | custom-call | tf_op jit(solution)/shard_map/pallas_call | solution.py:530
  (40 shorter events, 0.2 us)
Async XLA Ops:
  1.0 5.9 %copy-start.5 = (f32[3,5,16,128]{3,2,1,0:T(8,128)}, f32[3,5,16,128]{3,2,1,0:T(8,128)S(1)}, u32[]{:S(2)}) copy-start(f32[3,5,16,128]{3,2,1,0:T(8,128)S(1)} %get-tuple-element.136) | copy-start | bytes 368644
  1.0 5.9 %copy-start.6 = (f32[3,5,16,128]{3,2,1,0:T(8,128)}, f32[3,5,16,128]{3,2,1,0:T(8,128)S(1)}, u32[]{:S(2)}) copy-start(f32[3,5,16,128]{3,2,1,0:T(8,128)S(1)} %get-tuple-element.137) | copy-start | bytes 368644
  1.0 11.3 %collective-permute-start = (f32[3,80,128]{2,1,0:T(8,128)S(1)}, f32[3,80,128]{2,1,0:T(8,128)S(1)}, u32[]{:S(2)}, u32[]{:S(2)}) collective-permute-start(f32[3,80,128]{2,1,0:T(8,128)S(1)} %bitcast.15), channel_id=1, source_target_pairs={{0,1},{1,2},{2,3},{3,4},{4,5},{5,6},{6,7},{7,0},{8,9},{9,10},{10,1... | collective-permute-start | bytes 368648 | tf_op jit(solution)/shard_map/ppermute | solution.py:599
  2.6 9.7 %collective-permute-start.1 = (f32[3,80,128]{2,1,0:T(8,128)S(1)}, f32[3,80,128]{2,1,0:T(8,128)S(1)}, u32[]{:S(2)}, u32[]{:S(2)}) collective-permute-start(f32[3,80,128]{2,1,0:T(8,128)S(1)} %bitcast.13), channel_id=1, source_target_pairs={{1,0},{2,1},{3,2},{4,3},{5,4},{6,5},{7,6},{0,7},{9,8},{10,9},{11,1... | collective-permute-start | bytes 368648 | tf_op jit(solution)/shard_map/ppermute | solution.py:600
  12.0 8.3 %copy-start.4 = (f32[360,1536]{1,0:T(8,128)S(1)}, f32[360,1536]{1,0:T(8,128)}, u32[]{:S(2)}) copy-start(f32[360,1536]{1,0:T(8,128)} %constant.49.clone) | copy-start | bytes 6635524
  12.1 8.3 %copy-start.9 = (f32[360]{0:T(512)S(1)}, f32[360]{0:T(512)}, u32[]{:S(2)}) copy-start(f32[360]{0:T(512)} %constant.54) | copy-start | bytes 4324
  12.1 8.3 %copy-start.10 = (f32[360]{0:T(512)S(1)}, f32[360]{0:T(512)}, u32[]{:S(2)}) copy-start(f32[360]{0:T(512)} %constant.48.clone) | copy-start | bytes 4324
  12.3 9.3 %copy-start = (f32[3,80,128]{2,1,0:T(8,128)}, f32[3,80,128]{2,1,0:T(8,128)S(1)}, u32[]{:S(2)}) copy-start(f32[3,80,128]{2,1,0:T(8,128)S(1)} %collective-permute-done.west_ref) | copy-start | bytes 368644
  12.3 9.2 %copy-start.1 = (f32[3,80,128]{2,1,0:T(8,128)}, f32[3,80,128]{2,1,0:T(8,128)S(1)}, u32[]{:S(2)}) copy-start(f32[3,80,128]{2,1,0:T(8,128)S(1)} %collective-permute-done.1.east_ref) | copy-start | bytes 368644
  14.2 7.3 %copy-start.3 = (f32[361,1536]{1,0:T(8,128)S(1)}, f32[361,1536]{1,0:T(8,128)}, u32[]{:S(2)}) copy-start(f32[361,1536]{1,0:T(8,128)} %constant.47.clone) | copy-start | bytes 6653956
  14.3 7.3 %copy-start.7 = (f32[361]{0:T(512)S(1)}, f32[361]{0:T(512)}, u32[]{:S(2)}) copy-start(f32[361]{0:T(512)} %constant.53) | copy-start | bytes 4336
  14.3 7.3 %copy-start.8 = (f32[361]{0:T(512)S(1)}, f32[361]{0:T(512)}, u32[]{:S(2)}) copy-start(f32[361]{0:T(512)} %constant.46.clone) | copy-start | bytes 4336
  14.3 35.3 %collective-permute-start.3 = (f32[13,200,128]{2,1,0:T(8,128)}, f32[13,200,128]{2,1,0:T(8,128)}, u32[]{:S(2)}, u32[]{:S(2)}) collective-permute-start(f32[13,200,128]{2,1,0:T(8,128)} %get-tuple-element.127._), channel_id=1, source_target_pairs={{8,0},{16,8},{24,16},{32,24},{40,32},{48,40},{56,48},{64,56},{72,6... | collective-permute-start | bytes 3993608 | tf_op jit(solution)/shard_map/ppermute | solution.py:619
  18.4 31.2 %collective-permute-start.2 = (f32[13,200,128]{2,1,0:T(8,128)}, f32[13,200,128]{2,1,0:T(8,128)}, u32[]{:S(2)}, u32[]{:S(2)}) collective-permute-start(f32[13,200,128]{2,1,0:T(8,128)} %get-tuple-element.130), channel_id=1, source_target_pairs={{0,8},{8,16},{16,24},{24,32},{32,40},{40,48},{48,56},{56,64},{64,7... | collective-permute-start | bytes 3993608 | tf_op jit(solution)/shard_map/ppermute | solution.py:618
  33.1 64.2 %collective-permute-start.4 = (f32[8,184,128]{2,1,0:T(8,128)}, f32[8,184,128]{2,1,0:T(8,128)S(1)}, u32[]{:S(2)}, u32[]{:S(2)}) collective-permute-start(f32[8,184,128]{2,1,0:T(8,128)} %get-tuple-element.131), channel_id=1, source_target_pairs={{0,32},{8,40},{16,48},{24,56},{96,64},{104,72},{112,80},{120,88},{... | collective-permute-start | bytes 2261000 | tf_op jit(solution)/shard_map/ppermute | solution.py:622
  35.5 63.1 %collective-permute-start.5 = (f32[8,184,128]{2,1,0:T(8,128)}, f32[8,184,128]{2,1,0:T(8,128)}, u32[]{:S(2)}, u32[]{:S(2)}) collective-permute-start(f32[8,184,128]{2,1,0:T(8,128)} %get-tuple-element.132), channel_id=1, source_target_pairs={{0,32},{8,40},{16,48},{24,56},{96,64},{104,72},{112,80},{120,88},{... | collective-permute-start | bytes 2261000 | tf_op jit(solution)/shard_map/ppermute | solution.py:623
  97.3 48.2 %collective-permute-start.6 = (f32[8,184,128]{2,1,0:T(8,128)}, f32[8,184,128]{2,1,0:T(8,128)S(1)}, u32[]{:S(2)}, u32[]{:S(2)}) collective-permute-start(f32[8,184,128]{2,1,0:T(8,128)} %get-tuple-element.141), channel_id=1, source_target_pairs={{32,0},{40,8},{48,16},{56,24},{64,96},{72,104},{80,112},{88,120},{... | collective-permute-start | bytes 2261000 | tf_op jit(solution)/shard_map/ppermute | solution.py:647
  98.7 46.9 %collective-permute-start.7 = (f32[8,184,128]{2,1,0:T(8,128)S(1)}, f32[8,184,128]{2,1,0:T(8,128)S(1)}, u32[]{:S(2)}, u32[]{:S(2)}) collective-permute-start(f32[8,184,128]{2,1,0:T(8,128)S(1)} %get-tuple-element.139._), channel_id=1, source_target_pairs={{32,0},{40,8},{48,16},{56,24},{64,96},{72,104},{80,112},{88,120},{... | collective-permute-start | bytes 2261000 | tf_op jit(solution)/shard_map/ppermute | solution.py:649

commit v4 on v3

--- a/solution.py
+++ b/solution.py
@@ -596,8 +596,8 @@
     flat = state.reshape(3, cols * rows, lev)
     last = state[:, cols - HALO :].reshape(3, HALO * rows, lev)
     first = state[:, :HALO].reshape(3, HALO * rows, lev)
+    east_ = lax.ppermute(first, "lon", left)
     west = lax.ppermute(last, "lon", right)
-    east_ = lax.ppermute(first, "lon", left)
     outward = [(b, b + quarter) for b in range(quarter)]
     outward += [(b, b - quarter) for b in range(lat_count - quarter, lat_count)]
     inward = [(j, i) for i, j in outward]

time: 151 us -> 151 us (level)
  no operation moved by 1% of the time
where the time goes in v4:
time: 151 us
  blocking collectives  78.9 us (52%)
  Pallas kernels  39.4 us (26%)
  starting transfers between devices  18.3 us (12%)
  waiting for transfers between devices  8.55 us (6%)
  matrix products  2.33 us (2%)
  local copies, waits for them, and re-layouts  1.69 us (1%)
    all_to_all x2, blocking collectives, swapped(): return lax.all_to_all(x, 'lon', split_axis=0, concat_axis=0, tiled=True)  78.9 us
    pallas_call x1, Pallas kernels, inner_rows(): pl.pallas_call(functools.partial(inner_kernel, cols, rows), in_specs=[sme...  9.67 us
    ppermute x1, waiting for transfers between devices, body(): halo_north = lax.ppermute(send_south, 'lat', up)  8.53 us
    pallas_call x1, Pallas kernels, filtered(): pl.pallas_call(functools.partial(filter_kernel, groups, cols), in_specs=[...  7.19 us
    pallas_call x1, Pallas kernels, edge_rows(): pl.pallas_call(functools.partial(edge_kernel, cols, rows, near_pole), in_...  7.08 us
    pallas_call x1, Pallas kernels, joined(): pl.pallas_call(functools.partial(join_kernel, cols, rows), in_specs=[smem...  5.13 us
    pallas_call x1, Pallas kernels, split_planes(): pl.pallas_call(functools.partial(split_kernel, cols, rows), in_specs=[any...  5.13 us
    ppermute x1, starting transfers between devices, body(): halo_south = lax.ppermute(send_north, 'lat', down)  4.11 us
  transfers between devices with their start and end apart: 8, of which 1 were waited for; matrix products, arithmetic and copies ran while one was open for 3% of the time, Pallas kernels for 21%

profile of v4, /device:TPU:24, one launch (start us, length us, event | category | flops | bytes accessed | tf_op | source)
XLA Modules:
  0.0 150.8 jit_solution(9547253578011436351)
XLA Ops:
  0.0 1.0 fusion.14
  1.0 1.6 %collective-permute-start = (f32[3,80,128]{2,1,0:T(8,128)S(1)}, f32[3,80,128]{2,1,0:T(8,128)S(1)}, u32[]{:S(2)}, u32[]{:S(2)}) collective-permute-start(f32[3,80,128]{2,1,0:T(8,128)S(1)} %bitcast.15), channel_id=1, source_target_pairs={{0,1},{1,2},{2,3},{3,4},{4,5},{5,6},{6,7},{7,0},{8,9},{9,10},{10,1... | collective-permute-start | bytes 368648 | tf_op jit(solution)/shard_map/ppermute | solution.py:600
  2.6 3.6 %collective-permute-start.1 = (f32[3,80,128]{2,1,0:T(8,128)S(1)}, f32[3,80,128]{2,1,0:T(8,128)S(1)}, u32[]{:S(2)}, u32[]{:S(2)}) collective-permute-start(f32[3,80,128]{2,1,0:T(8,128)S(1)} %bitcast.13), channel_id=1, source_target_pairs={{1,0},{2,1},{3,2},{4,3},{5,4},{6,5},{7,6},{0,7},{9,8},{10,9},{11,1... | collective-permute-start | bytes 368648 | tf_op jit(solution)/shard_map/ppermute | solution.py:599
  6.2 0.1 pad_add_fusion.1
  6.2 0.7 convert_element_type.16
  6.9 5.1 %shard_map.64 = (f32[3,16,200,128]{3,2,1,0:T(8,128)}, f32[13,200,128]{2,1,0:T(8,128)}, f32[13,200,128]{2,1,0:T(8,128)}) custom-call(f32[3,2880,128]{2,1,0:T(8,128)} %bitcast.12, f32[3,80,128]{2,1,0:T(8,128)} %bitcast.16, f32[3,80,128]{2,1,0:T(8,128)} %bitcast.14), custom_call_target="tpu_custom_call" | custom-call | tf_op jit(solution)/shard_map/pallas_call | solution.py:96
  12.0 0.0 copy-start.4
  12.1 0.0 copy-start.9
  12.1 0.0 copy-start.10
  12.1 0.2 fusion.11.x_ref
  12.3 1.9 %shard_map.65 = (f32[13,200,128]{2,1,0:T(8,128)}, f32[13,200,128]{2,1,0:T(8,128)}) custom-call(f32[3,80,128]{2,1,0:T(8,128)S(1)} %collective-permute-done.west_ref, f32[3,80,128]{2,1,0:T(8,128)S(1)} %collective-permute-done.1.east_ref, f32[13,200,128]{2,1,0:T(8,128)} %get-tuple-element.125._, ...), custom_call_target="tpu_custom_call", output_to_operand_aliasing={{0}: (2, {}), {1}: (3, {})} | custom-call | tf_op jit(solution)/shard_map/pallas_call | solution.py:135
  14.2 0.0 copy-start.3
  14.3 4.1 %collective-permute-start.3 = (f32[13,200,128]{2,1,0:T(8,128)}, f32[13,200,128]{2,1,0:T(8,128)}, u32[]{:S(2)}, u32[]{:S(2)}) collective-permute-start(f32[13,200,128]{2,1,0:T(8,128)} %get-tuple-element.127._), channel_id=1, source_target_pairs={{8,0},{16,8},{24,16},{32,24},{40,32},{48,40},{56,48},{64,56},{72,6... | collective-permute-start | bytes 3993608 | tf_op jit(solution)/shard_map/ppermute | solution.py:619
  18.4 1.9 %collective-permute-start.2 = (f32[13,200,128]{2,1,0:T(8,128)}, f32[13,200,128]{2,1,0:T(8,128)}, u32[]{:S(2)}, u32[]{:S(2)}) collective-permute-start(f32[13,200,128]{2,1,0:T(8,128)} %get-tuple-element.130), channel_id=1, source_target_pairs={{0,8},{8,16},{16,24},{24,32},{32,40},{40,48},{48,56},{56,64},{64,7... | collective-permute-start | bytes 3993608 | tf_op jit(solution)/shard_map/ppermute | solution.py:618
  20.4 1.2 fusion.1
  21.6 1.2 fusion.2
  22.8 0.6 reshape_squeeze.3.off_ref
  23.4 9.7 %shard_map.67 = (f32[8,184,128]{2,1,0:T(8,128)}, f32[8,184,128]{2,1,0:T(8,128)}, f32[8,184,128]{2,1,0:T(8,128)}, f32[3,10,200,128]{3,2,1,0:T(8,128)}, f32[3,4,200,128]{3,2,1,0:T(8,128)}) custom-call(f32[26]{0:T(128)S(1)} %maximum_divide_fusion.metric_ref, f32[3,16,200,128]{3,2,1,0:T(8,128)} %get-tuple-element.124.planes_ref, f32[3,80,128]{2,1,0:T(8,128)} %copy-done, ...), custom_call_target="tpu_custom_call" | custom-call | bytes 33210000 | tf_op jit(solution)/shard_map/pallas_call | solution.py:241
  33.1 2.4 %collective-permute-start.4 = (f32[8,184,128]{2,1,0:T(8,128)}, f32[8,184,128]{2,1,0:T(8,128)S(1)}, u32[]{:S(2)}, u32[]{:S(2)}) collective-permute-start(f32[8,184,128]{2,1,0:T(8,128)} %get-tuple-element.131), channel_id=1, source_target_pairs={{0,32},{8,40},{16,48},{24,56},{96,64},{104,72},{112,80},{120,88},{... | collective-permute-start | bytes 2261000 | tf_op jit(solution)/shard_map/ppermute | solution.py:622
  35.5 2.2 %collective-permute-start.5 = (f32[8,184,128]{2,1,0:T(8,128)}, f32[8,184,128]{2,1,0:T(8,128)}, u32[]{:S(2)}, u32[]{:S(2)}) collective-permute-start(f32[8,184,128]{2,1,0:T(8,128)} %get-tuple-element.132), channel_id=1, source_target_pairs={{0,32},{8,40},{16,48},{24,56},{96,64},{104,72},{112,80},{120,88},{... | collective-permute-start | bytes 2261000 | tf_op jit(solution)/shard_map/ppermute | solution.py:623
  37.7 0.1 pad_add_fusion.ids_ref
  37.8 3.3 %shard_map.68 = (bf16[2,2,128,1408]{3,2,1,0:T(8,128)(2,1)}, bf16[2,2,128,1408]{3,2,1,0:T(8,128)(2,1)}) custom-call(f32[2,2,1,1536]{3,2,1,0:T(1,128)S(1)} %broadcast_in_dim.39.p_ref, f32[8,128]{1,0:T(8,128)S(1)} %broadcast_in_dim.40._.x_ref), custom_call_target="tpu_custom_call" | custom-call | tf_op jit(solution)/shard_map/pallas_call | solution.py:434
  41.1 8.5 %collective-permute-done.2 = f32[13,200,128]{2,1,0:T(8,128)} collective-permute-done((f32[13,200,128]{2,1,0:T(8,128)}, f32[13,200,128]{2,1,0:T(8,128)}, u32[]{:S(2)}, u32[]{:S(2)}) %collective-permute-start.2) | collective-permute-done | bytes 1331232 | tf_op jit(solution)/shard_map/ppermute | solution.py:618
  49.6 47.7 %conditional.5 = (f32[8,736,128]{2,1,0:T(8,128)}) conditional(s32[]{:T(128)} %convert_element_type.6, () %tuple.35, (s32[4]{0:T(128)S(1)}, f32[26]{0:T(128)S(1)}, f32[3,4,200,128]{3,2,1,0:T(8,128)}, f32[3,10,200,128]{3,2,1,0:T(8,128)}, f32[13,200,128]{2,1,0:T(8,128)}, /*index=5*/f32[13,200,128]{2,1,0:T(8,128)}, f32[8,184,128]{2,1,0:T(8,128)}, ...), branch_computations={%region_1.2_spmd, %region_2.3_spmd} | conditional | bytes 6029320 | solution.py:645
  49.6 7.1 %branch_1_fun.5 = f32[8,736,128]{2,1,0:T(8,128)} custom-call(s32[4]{0:T(128)S(1)} %get-tuple-element.76.ids_ref, f32[26]{0:T(128)S(1)} %get-tuple-element.78.refs_0_, f32[3,4,200,128]{3,2,1,0:T(8,128)} %get-tuple-element.80.refs_1_, f32[3,10,200,128]{3,2,1,0:T(8,128)} %get-tuple-element.82.refs_2_, f32[13,200,128]{2,1,0:T(8,128)} %get-tuple-element.83.refs_3_, ...), custom_call_target="tpu_custom_call" | custom-call | tf_op jit(solution)/shard_map/cond/branch_1_fun/pallas_call | solution.py:348
  56.7 40.6 %all_to_all.24 = f32[8,736,128]{2,1,0:T(8,128)} all-to-all(f32[8,736,128]{2,1,0:T(8,128)} %branch_1_fun.5), channel_id=1, replica_groups=mesh['lat'=16,'lon'=8] {'lon'}, dimensions={0} | all-to-all | bytes 6029312 | tf_op jit(solution)/shard_map/cond/branch_1_fun/all_to_all | solution.py:576
  97.3 1.3 collective-permute-start.6
  98.7 1.3 collective-permute-start.7
  100.0 45.5 %conditional.7 = (f32[8,736,128]{2,1,0:T(8,128)}) conditional(s32[]{:T(128)} %convert_element_type.6, f32[8,736,128]{2,1,0:T(8,128)} %get-tuple-element.138._, (bf16[2,2,128,1408]{3,2,1,0:T(8,128)(2,1)}, bf16[2,2,128,1408]{3,2,1,0:T(8,128)(2,1)}, f32[8,736,128]{2,1,0:T(8,128)}, f32[8,128]{1,0:T(8,128)S(1)}) %tuple.39), branch_computations={%region_5.6_spmd, %region_6.7_spmd} | conditional | bytes 6029320 | solution.py:651
  100.0 7.2 %branch_1_fun.7 = f32[8,736,128]{2,1,0:T(8,128)S(1)} custom-call(bf16[2,2,128,1408]{3,2,1,0:T(8,128)(2,1)} %get-tuple-element.94.hi_ref, bf16[2,2,128,1408]{3,2,1,0:T(8,128)(2,1)} %get-tuple-element.95.lo_ref, f32[8,736,128]{2,1,0:T(8,128)} %get-tuple-element.96.x_ref, f32[8,128]{1,0:T(8,128)S(1)} %get-tuple-element.97._), custom_call_target="tpu_custom_call" | custom-call | tf_op jit(solution)/shard_map/cond/branch_1_fun/pallas_call | solution.py:497
  107.2 38.3 %all_to_all.26 = f32[8,736,128]{2,1,0:T(8,128)} all-to-all(f32[8,736,128]{2,1,0:T(8,128)S(1)} %branch_1_fun.7), channel_id=1, replica_groups=mesh['lat'=16,'lon'=8] {'lon'}, dimensions={0} | all-to-all | bytes 6029312 | tf_op jit(solution)/shard_map/cond/branch_1_fun/all_to_all | solution.py:576
  145.5 5.1 %shard_map.71 = f32[3,2880,128]{2,1,0:T(8,128)} custom-call(s32[4]{0:T(128)S(1)} %pad_add_fusion.ids_ref, f32[8,736,128]{2,1,0:T(8,128)} %get-tuple-element.140.y_ref, f32[8,184,128]{2,1,0:T(8,128)S(1)} %collective-permute-done.6.u_ref, f32[8,184,128]{2,1,0:T(8,128)S(1)} %collective-permute-done.7.v_ref, ...), custom_call_target="tpu_custom_call", output_to_operand_aliasing={{}: (4, {})} | custom-call | tf_op jit(solution)/shard_map/pallas_call | solution.py:530
  (40 shorter events, 0.2 us)
Async XLA Ops:
  1.0 5.9 %copy-start.5 = (f32[3,5,16,128]{3,2,1,0:T(8,128)}, f32[3,5,16,128]{3,2,1,0:T(8,128)S(1)}, u32[]{:S(2)}) copy-start(f32[3,5,16,128]{3,2,1,0:T(8,128)S(1)} %get-tuple-element.136) | copy-start | bytes 368644
  1.0 5.9 %copy-start.6 = (f32[3,5,16,128]{3,2,1,0:T(8,128)}, f32[3,5,16,128]{3,2,1,0:T(8,128)S(1)}, u32[]{:S(2)}) copy-start(f32[3,5,16,128]{3,2,1,0:T(8,128)S(1)} %get-tuple-element.137) | copy-start | bytes 368644
  1.0 11.3 %collective-permute-start = (f32[3,80,128]{2,1,0:T(8,128)S(1)}, f32[3,80,128]{2,1,0:T(8,128)S(1)}, u32[]{:S(2)}, u32[]{:S(2)}) collective-permute-start(f32[3,80,128]{2,1,0:T(8,128)S(1)} %bitcast.15), channel_id=1, source_target_pairs={{0,1},{1,2},{2,3},{3,4},{4,5},{5,6},{6,7},{7,0},{8,9},{9,10},{10,1... | collective-permute-start | bytes 368648 | tf_op jit(solution)/shard_map/ppermute | solution.py:600
  2.6 9.7 %collective-permute-start.1 = (f32[3,80,128]{2,1,0:T(8,128)S(1)}, f32[3,80,128]{2,1,0:T(8,128)S(1)}, u32[]{:S(2)}, u32[]{:S(2)}) collective-permute-start(f32[3,80,128]{2,1,0:T(8,128)S(1)} %bitcast.13), channel_id=1, source_target_pairs={{1,0},{2,1},{3,2},{4,3},{5,4},{6,5},{7,6},{0,7},{9,8},{10,9},{11,1... | collective-permute-start | bytes 368648 | tf_op jit(solution)/shard_map/ppermute | solution.py:599
  12.0 8.3 %copy-start.4 = (f32[360,1536]{1,0:T(8,128)S(1)}, f32[360,1536]{1,0:T(8,128)}, u32[]{:S(2)}) copy-start(f32[360,1536]{1,0:T(8,128)} %constant.49.clone) | copy-start | bytes 6635524
  12.1 8.3 %copy-start.9 = (f32[360]{0:T(512)S(1)}, f32[360]{0:T(512)}, u32[]{:S(2)}) copy-start(f32[360]{0:T(512)} %constant.54) | copy-start | bytes 4324
  12.1 8.3 %copy-start.10 = (f32[360]{0:T(512)S(1)}, f32[360]{0:T(512)}, u32[]{:S(2)}) copy-start(f32[360]{0:T(512)} %constant.48.clone) | copy-start | bytes 4324
  12.3 9.3 %copy-start = (f32[3,80,128]{2,1,0:T(8,128)}, f32[3,80,128]{2,1,0:T(8,128)S(1)}, u32[]{:S(2)}) copy-start(f32[3,80,128]{2,1,0:T(8,128)S(1)} %collective-permute-done.west_ref) | copy-start | bytes 368644
  12.3 9.2 %copy-start.1 = (f32[3,80,128]{2,1,0:T(8,128)}, f32[3,80,128]{2,1,0:T(8,128)S(1)}, u32[]{:S(2)}) copy-start(f32[3,80,128]{2,1,0:T(8,128)S(1)} %collective-permute-done.1.east_ref) | copy-start | bytes 368644
  14.2 7.3 %copy-start.3 = (f32[361,1536]{1,0:T(8,128)S(1)}, f32[361,1536]{1,0:T(8,128)}, u32[]{:S(2)}) copy-start(f32[361,1536]{1,0:T(8,128)} %constant.47.clone) | copy-start | bytes 6653956
  14.3 7.3 %copy-start.7 = (f32[361]{0:T(512)S(1)}, f32[361]{0:T(512)}, u32[]{:S(2)}) copy-start(f32[361]{0:T(512)} %constant.53) | copy-start | bytes 4336
  14.3 7.3 %copy-start.8 = (f32[361]{0:T(512)S(1)}, f32[361]{0:T(512)}, u32[]{:S(2)}) copy-start(f32[361]{0:T(512)} %constant.46.clone) | copy-start | bytes 4336
  14.3 35.3 %collective-permute-start.3 = (f32[13,200,128]{2,1,0:T(8,128)}, f32[13,200,128]{2,1,0:T(8,128)}, u32[]{:S(2)}, u32[]{:S(2)}) collective-permute-start(f32[13,200,128]{2,1,0:T(8,128)} %get-tuple-element.127._), channel_id=1, source_target_pairs={{8,0},{16,8},{24,16},{32,24},{40,32},{48,40},{56,48},{64,56},{72,6... | collective-permute-start | bytes 3993608 | tf_op jit(solution)/shard_map/ppermute | solution.py:619
  18.4 31.2 %collective-permute-start.2 = (f32[13,200,128]{2,1,0:T(8,128)}, f32[13,200,128]{2,1,0:T(8,128)}, u32[]{:S(2)}, u32[]{:S(2)}) collective-permute-start(f32[13,200,128]{2,1,0:T(8,128)} %get-tuple-element.130), channel_id=1, source_target_pairs={{0,8},{8,16},{16,24},{24,32},{32,40},{40,48},{48,56},{56,64},{64,7... | collective-permute-start | bytes 3993608 | tf_op jit(solution)/shard_map/ppermute | solution.py:618
  33.1 64.2 %collective-permute-start.4 = (f32[8,184,128]{2,1,0:T(8,128)}, f32[8,184,128]{2,1,0:T(8,128)S(1)}, u32[]{:S(2)}, u32[]{:S(2)}) collective-permute-start(f32[8,184,128]{2,1,0:T(8,128)} %get-tuple-element.131), channel_id=1, source_target_pairs={{0,32},{8,40},{16,48},{24,56},{96,64},{104,72},{112,80},{120,88},{... | collective-permute-start | bytes 2261000 | tf_op jit(solution)/shard_map/ppermute | solution.py:622
  35.5 63.1 %collective-permute-start.5 = (f32[8,184,128]{2,1,0:T(8,128)}, f32[8,184,128]{2,1,0:T(8,128)}, u32[]{:S(2)}, u32[]{:S(2)}) collective-permute-start(f32[8,184,128]{2,1,0:T(8,128)} %get-tuple-element.132), channel_id=1, source_target_pairs={{0,32},{8,40},{16,48},{24,56},{96,64},{104,72},{112,80},{120,88},{... | collective-permute-start | bytes 2261000 | tf_op jit(solution)/shard_map/ppermute | solution.py:623
  97.3 48.2 %collective-permute-start.6 = (f32[8,184,128]{2,1,0:T(8,128)}, f32[8,184,128]{2,1,0:T(8,128)S(1)}, u32[]{:S(2)}, u32[]{:S(2)}) collective-permute-start(f32[8,184,128]{2,1,0:T(8,128)} %get-tuple-element.141), channel_id=1, source_target_pairs={{32,0},{40,8},{48,16},{56,24},{64,96},{72,104},{80,112},{88,120},{... | collective-permute-start | bytes 2261000 | tf_op jit(solution)/shard_map/ppermute | solution.py:647
  98.7 46.9 %collective-permute-start.7 = (f32[8,184,128]{2,1,0:T(8,128)S(1)}, f32[8,184,128]{2,1,0:T(8,128)S(1)}, u32[]{:S(2)}, u32[]{:S(2)}) collective-permute-start(f32[8,184,128]{2,1,0:T(8,128)S(1)} %get-tuple-element.139._), channel_id=1, source_target_pairs={{32,0},{40,8},{48,16},{56,24},{64,96},{72,104},{80,112},{88,120},{... | collective-permute-start | bytes 2261000 | tf_op jit(solution)/shard_map/ppermute | solution.py:649
